TPU v7x, 32 devices: a whole 2x2x4 slice. The times are simulated.
32 devices in a mesh: frame: 8 (over y, x, core), video: 4 (over z).
Axes of the slice: x: 2, y: 2, z: 4, core: 2. Of those that a mesh axis runs over, the one named last changes fastest.
Arguments:
- tokens: bfloat16 [12, 16, 197, 768], P('video', 'frame'), may hold values from -6 to 6
- cotangent: bfloat16 [12, 16, 197, 768], P('video', 'frame'), may hold values from -6 to 6
- msg_weight: bfloat16 [768, 768], replicated, may hold values from -0.21875 to 0.21875
- msg_bias: bfloat16 [768], replicated, may hold values from -1.75 to 1.75
- msg_norm_gain: bfloat16 [768], replicated, may hold values from 0.5 to 1.5
- msg_norm_shift: bfloat16 [768], replicated, may hold values from -1.75 to 1.75
- msg_in_weight: bfloat16 [768, 2304], replicated, may hold values from -0.21875 to 0.21875
- msg_in_bias: bfloat16 [1536], replicated, may hold values from -1.75 to 1.75
- msg_out_weight: bfloat16 [768, 768], replicated, may hold values from -0.4375 to 0.4375
- msg_out_bias: bfloat16 [768], replicated, may hold values from -1.75 to 1.75
- norm1_gain: bfloat16 [768], replicated, may hold values from 0.5 to 1.5
- norm1_shift: bfloat16 [768], replicated, may hold values from -1.75 to 1.75
- attn_in_weight: bfloat16 [768, 2304], replicated, may hold values from -0.21875 to 0.21875
- attn_in_bias: bfloat16 [1536], replicated, may hold values from -1.75 to 1.75
- attn_out_weight: bfloat16 [768, 768], replicated, may hold values from -1.25 to 1.25
- attn_out_bias: bfloat16 [768], replicated, may hold values from -1.75 to 1.75
- norm2_gain: bfloat16 [768], replicated, may hold values from 0.5 to 1.5
- norm2_shift: bfloat16 [768], replicated, may hold values from -1.75 to 1.75
- fc_weight: bfloat16 [768, 3072], replicated, may hold values from -0.21875 to 0.21875
- fc_bias: bfloat16 [3072], replicated, may hold values from -1.75 to 1.75
- proj_weight: bfloat16 [3072, 768], replicated, may hold values from -0.109375 to 0.109375
- proj_bias: bfloat16 [768], replicated, may hold values from -1.75 to 1.75
Outputs:
- output: bfloat16 [12, 16, 197, 768], P('video', 'frame')
- tokens_grad: float32 [12, 16, 197, 768], P('video', 'frame')
- msg_weight_grad: float32 [768, 768], P('frame', 'video')
- msg_bias_grad: float32 [768], P('frame')
- msg_norm_gain_grad: float32 [768], P('frame')
- msg_norm_shift_grad: float32 [768], P('frame')
- msg_in_weight_grad: float32 [768, 2304], P('frame', 'video')
- msg_in_bias_grad: float32 [1536], P('frame')
- msg_out_weight_grad: float32 [768, 768], P('frame', 'video')
- msg_out_bias_grad: float32 [768], P('frame')
- norm1_gain_grad: float32 [768], P('frame')
- norm1_shift_grad: float32 [768], P('frame')
- attn_in_weight_grad: float32 [768, 2304], P('frame', 'video')
- attn_in_bias_grad: float32 [1536], P('frame')
- attn_out_weight_grad: float32 [768, 768], P('frame', 'video')
- attn_out_bias_grad: float32 [768], P('frame')
- norm2_gain_grad: float32 [768], P('frame')
- norm2_shift_grad: float32 [768], P('frame')
- fc_weight_grad: float32 [768, 3072], P('frame', 'video')
- fc_bias_grad: float32 [3072], P('frame')
- proj_weight_grad: float32 [3072, 768], P('frame', 'video')
- proj_bias_grad: float32 [768], P('frame')
All inputs are finite; a program needn't handle non-finite values.
Results may differ from a plain program's by a relative error of at most 0.025.
Values may be sent and summed in bfloat16 or wider, within the bound.
A program may use at most 192 MiB of HBM per device.

v0:
```python
import functools
import math

import jax
import jax.numpy as jnp
from jax import lax
from jax.experimental import pallas as pl
from jax.experimental.pallas import tpu as pltpu
from jax.sharding import PartitionSpec as P

D = 768
HEADS = 12
PAIRS = 6
FF = 3072
PATCHES = 197
JOINED = 198
ROWS = 208
KEYS = 256
HALF = D // 2
FRAMES = 16
BLOCK = 192
UNITS = 3
BF = jnp.bfloat16
F32 = jnp.float32
MIB = 1 << 20
MESH = pl.DeviceIdType.MESH


def vec(ref, at=0):
    return ref[...].astype(F32).reshape(1, ref.shape[0])[:, at * D : at * D + D]


def dims(a, b, ca, cb):
    return lax.dot_general(a, b, (((ca,), (cb,)), ((), ())), preferred_element_type=F32)


def column_sum(x):
    return jnp.sum(x, axis=0, keepdims=True)


def norm_fwd(x, gain, shift):
    centre = x - jnp.mean(x, axis=-1, keepdims=True)
    inv = lax.rsqrt(jnp.mean(centre * centre, axis=-1, keepdims=True) + 1e-05)
    unit = centre * inv
    return unit * gain + shift, unit, inv


def norm_back(grad, unit, inv, gain):
    scaled = grad * gain
    return inv * (
        scaled
        - jnp.mean(scaled, axis=-1, keepdims=True)
        - unit * jnp.mean(scaled * unit, axis=-1, keepdims=True)
    )


def low_half():
    return lax.broadcasted_iota(jnp.int32, (1, 128), 1) < 64


def half(low, head, value, other):
    return jnp.where(low, value, other) if head == 0 else jnp.where(low, other, value)


def pair_fwd(q, k, v, mask_scores, keep):
    low = low_half()
    sums = []
    for head in range(2):
        scores = mask_scores(dims(q, half(low, head, k, jnp.zeros_like(k)), 1, 1))
        top = jnp.max(scores, axis=1, keepdims=True)
        probs = jnp.exp(scores - top).astype(BF)
        keep(head, probs)
        sums.append(dims(probs, half(low, head, v, jnp.ones_like(v)), 1, 0))
    inv = 1.0 / pltpu.roll(jnp.where(low, sums[1], sums[0]), 64, 1)
    return jnp.where(low, sums[0], sums[1]) * inv, inv


def pair_back(q, k, v, grad, mixed, inv, probs):
    low = low_half()
    scaled = grad * inv
    scaled_low = scaled.astype(BF)
    both = mixed.astype(F32) * scaled
    zero = jnp.zeros_like(both)
    totals = None
    for head in range(2):
        p = probs(head)
        grad_p = dims(scaled_low, half(low, head, v, jnp.zeros_like(v)), 1, 1)
        delta = jnp.sum(half(low, head, both, zero), axis=1, keepdims=True)
        grad_s = (p.astype(F32) * (grad_p - delta)).astype(BF)
        terms = (
            dims(grad_s, half(low, head, k, jnp.zeros_like(k)), 1, 0),
            dims(grad_s, half(low, head, q, jnp.zeros_like(q)), 0, 0),
            dims(p, half(low, head, scaled_low, jnp.zeros_like(scaled_low)), 0, 0),
        )
        totals = terms if totals is None else tuple(a + b for a, b in zip(totals, terms))
    return totals[0] * 0.125, totals[1], totals[2]


def lanes(pair):
    return slice(pair * 128, pair * 128 + 128)


def msg_mask(rows):
    row = lax.broadcasted_iota(jnp.int32, (rows, rows), 0) // FRAMES
    col = lax.broadcasted_iota(jnp.int32, (rows, rows), 1) // FRAMES
    same = row == col
    return lambda scores: jnp.where(same, scores, -1e30)


def msg_scratch(rows):
    return [
        pltpu.VMEM((rows, 3 * D), BF), pltpu.VMEM((HEADS, rows, rows), BF), pltpu.VMEM((rows, D), F32), pltpu.VMEM((rows, D), BF),
        pltpu.VMEM((rows, D), BF), pltpu.VMEM((rows, D), F32),
    ]


def pair_lanes(pair, kind=0):
    return pl.ds(pl.multiple_of(kind * D + pair * 128, 128), 128)


def msg_forward(cls, biases, w_msg, w_in, w_out, scratch, unroll):
    bias, gain, shift, in_bias, _ = biases
    qkv, probs, invs, mixed, normed_low, message = scratch
    message[...] = dims(cls, w_msg[...], 1, 0) + vec(bias)
    normed, unit, inv_std = norm_fwd(message[...], vec(gain), vec(shift))
    normed_low[...] = normed.astype(BF)

    def project(kind, bias, scale):
        columns = slice(kind * D, kind * D + D)
        qkv[:, columns] = ((dims(normed_low[...], w_in[:, columns], 1, 0) + bias) * scale).astype(BF)

    project(0, vec(in_bias), 0.125)
    project(1, 0.0, 1.0)
    project(2, vec(in_bias, 1), 1.0)
    mask = msg_mask(cls.shape[0])

    @pl.loop(0, PAIRS, unroll=unroll)
    def _(pair):
        def keep(head, p):
            probs[2 * pair + head] = p

        out, inv = pair_fwd(qkv[:, pair_lanes(pair)], qkv[:, pair_lanes(pair, 1)], qkv[:, pair_lanes(pair, 2)], mask, keep)
        mixed[:, pair_lanes(pair)] = out.astype(BF)
        invs[:, pair_lanes(pair)] = inv

    return unit, inv_std


class Place:
    def __init__(self, frame_size, video_size):
        self.F, self.V = frame_size, video_size
        self.f, self.v = lax.axis_index("frame"), lax.axis_index("video")
        self.core = lax.rem(self.f, 2)
        self.bits = [lax.rem(lax.div(self.f, 1 << i), 2) for i in range(int(math.log2(frame_size)))]

    def frame_peer(self, step):
        return {"frame": lax.rem(self.f + step, self.F)}

    def video_peer(self, step):
        return {"video": lax.rem(self.v + step, self.V)}

    def greet(self):
        self.announce()
        self.meet()

    def announce(self):
        barrier = pltpu.get_barrier_semaphore()

        @pl.loop(1, self.F)
        def _(step):
            pl.semaphore_signal(barrier, inc=1, device_id=self.frame_peer(step), device_id_type=MESH)

        @pl.loop(1, self.V)
        def _(step):
            pl.semaphore_signal(barrier, inc=1, device_id=self.video_peer(step), device_id_type=MESH)

    def meet(self):
        pl.semaphore_wait(pltpu.get_barrier_semaphore(), self.F + self.V - 2)


def remote(src, dst, send, recv, peer):
    return pltpu.make_async_remote_copy(
        src_ref=src, dst_ref=dst, send_sem=send, recv_sem=recv, device_id=peer, device_id_type=MESH
    )


class Gather:
    def __init__(self, place, own, rows, send, recv):
        self.place, self.own, self.rows, self.send, self.recv = place, own, rows, send, recv

    def near_copy(self, step, arriving):
        place = self.place
        frame = lax.rem(place.f + place.F - step, place.F) if arriving else place.f
        return remote(
            self.own, self.rows.at[place.v, :, frame], self.send.at[0, step], self.recv.at[0, step], place.frame_peer(step)
        )

    def far_copy(self, hop, arriving):
        place = self.place
        video = lax.rem(place.v + place.V - hop, place.V) if arriving else place.v
        slot = place.F - 1 + hop
        return remote(
            self.own, self.rows.at[video, :, place.f], self.send.at[0, slot], self.recv.at[0, slot], place.video_peer(hop)
        )

    def passed_copy(self, hop, step, arriving):
        place = self.place
        video = lax.rem(place.v + place.V - hop, place.V)
        frame = lax.rem(place.f + place.F - step, place.F) if arriving else place.f
        part = self.rows.at[video, :, frame]
        return remote(part, part, self.send.at[hop, step], self.recv.at[hop, step], place.frame_peer(step))

    def each_frame(self, call):
        pl.loop(1, self.place.F)(call)

    def each_video(self, call):
        pl.loop(1, self.place.V)(call)

    def start(self, far=True):
        self.each_frame(lambda step: self.near_copy(step, False).start())
        self.each_video(lambda hop: self.far_copy(hop, False).start())

    def near(self):
        self.each_frame(lambda step: self.near_copy(step, True).wait_recv())

    def forward(self):
        @pl.loop(1, self.place.V)
        def _(hop):
            self.far_copy(hop, True).wait_recv()
            self.each_frame(lambda step: self.passed_copy(hop, step, False).start())

    def finish(self):
        @pl.loop(1, self.place.V)
        def _(hop):
            def passed(step):
                self.passed_copy(hop, step, True).wait_recv()
                self.passed_copy(hop, step, False).wait_send()

            self.each_frame(passed)
            self.far_copy(hop, False).wait_send()

        self.each_frame(lambda step: self.near_copy(step, False).wait_send())


def attn_fwd_kernel(
    frame_size, video_size, frames_here, videos_here,
    x_ref, x_hbm, gain1, shift1, in_bias1, out_bias1, w_in1, w_out_hbm, *rest,
):
    operands, rest = rest[:8], rest[8:]
    (
        q_hbm, k_hbm, v_hbm, normed_hbm, p_ref, inv_ref, mixed_ref, kept_ref, out_ref, cls_ref,
        q_ref, k_ref, v_ref, normed_ref, joined, w_out1, msg_rows, msg_wide, own, rows, wide, mixed_out, *rest,
    ) = rest
    kept, scratch, (send, recv, local, s_out) = rest[:8], rest[8:14], rest[14:]
    bias, gain, shift, in_bias, out_bias, w_msg, w_in, w_out = kept
    place = Place(frame_size, video_size)
    t = pl.program_id(0)
    i = lax.rem(t, videos_here)
    frames = videos_here * frames_here
    every = frames_here * ROWS
    gather = Gather(place, own, rows, send, recv)

    def loads():
        pairs = [(x_hbm.at[:, 0], own), (x_hbm.at[:, 0], rows.at[place.v, :, place.f]), (w_out_hbm, w_out1)]
        pairs += list(zip(operands, kept))
        return [pltpu.make_async_copy(source, target, local.at[at]) for at, (source, target) in enumerate(pairs)]

    def stores():
        pairs = ((q_ref, q_hbm), (k_ref, k_hbm), (v_ref, v_hbm), (normed_ref, normed_hbm))
        return [pltpu.make_async_copy(source, target, s_out.at[at]) for at, (source, target) in enumerate(pairs)]

    @pl.when(t == 0)
    def _():
        place.announce()
        for load in loads():
            load.start()

    @pl.when(t == min(1, videos_here - 1))
    def _():
        for load in loads()[:2]:
            load.wait()
        place.meet()
        gather.start()

    @pl.when(t < videos_here)
    def _():
        x = x_ref[0].astype(F32)
        first = i * frames_here
        for j in range(frames_here):
            joined[first + j, 0:PATCHES, :] = x[:, j, :]
            joined[first + j, PATCHES:ROWS, :] = jnp.zeros((ROWS - PATCHES, D), F32)
        here = pl.ds(first, frames_here)
        normed, _, _ = norm_fwd(joined[here].reshape(every, D), vec(gain1), vec(shift1))
        normed_ref[here] = normed.astype(BF).reshape(frames_here, ROWS, D)
        normed = normed_ref[here].reshape(every, D)
        pad = jnp.zeros((KEYS - ROWS, 128), BF)
        q = ((dims(normed, w_in1[:, :D], 1, 0) + vec(in_bias1)) * 0.125).astype(BF)
        k = dims(normed, w_in1[:, D : 2 * D], 1, 0).astype(BF)
        v = (dims(normed, w_in1[:, 2 * D :], 1, 0) + vec(in_bias1, 1)).astype(BF)
        for j in range(frames_here):
            part = slice(j * ROWS, j * ROWS + ROWS)
            for pair in range(PAIRS):
                sl = lanes(pair)
                q_ref[first + j, pair] = q[part, sl]
                k_ref[first + j, pair, 0:ROWS] = k[part, sl]
                k_ref[first + j, pair, ROWS:KEYS] = pad
                v_ref[first + j, pair, 0:ROWS] = v[part, sl]
                v_ref[first + j, pair, ROWS:KEYS] = pad

    def unpack(video):
        for n in range(videos_here):
            for f in range(frame_size):
                at = (n * frame_size + f) * frames_here
                wide[at : at + frames_here, :] = rows[video, n, f].astype(F32)

    @pl.when(t == videos_here)
    def _():
        gather.near()
        gather.forward()
        unpack(place.v)
        for load in loads()[2:]:
            load.wait()
        biases = (bias, gain, shift, in_bias, out_bias)
        msg_forward(wide[...].astype(BF), biases, w_msg, w_in, w_out, scratch, PAIRS)
        mixed_out[...] = scratch[5][...] + dims(scratch[3][...], w_out[...], 1, 0) + vec(out_bias)
        msg_rows[...] = jnp.zeros_like(msg_rows)
        for n in range(videos_here):
            for j in range(frames_here):
                c = n * frames_here + j
                row = mixed_out[pl.ds(n * FRAMES + place.f * frames_here + j, 1), :]
                out_ref[c] = row
                msg_rows[c : c + 1, :] = row
                joined[c, PATCHES : PATCHES + 1, :] = row
        normed, _, _ = norm_fwd(msg_rows[...], vec(gain1), vec(shift1))
        low = normed.astype(BF)
        msg_wide[:, :D] = low.astype(F32)
        msg_wide[:, D : 2 * D] = dims(low, w_in1[:, D : 2 * D], 1, 0)
        msg_wide[:, 2 * D :] = dims(low, w_in1[:, 2 * D :], 1, 0) + vec(in_bias1, 1)
        at = PATCHES - PATCHES % 16
        mine = lax.broadcasted_iota(jnp.int32, (16, 1), 0) == PATCHES % 16
        block = slice(at, at + 16)

        @pl.loop(0, frames)
        def _(c):
            row = msg_wide[pl.ds(c, 1), :]
            normed_ref[c, block, :] = jnp.where(mine, row[:, :D], normed_ref[c, block, :].astype(F32)).astype(BF)
            for pair in range(PAIRS):
                for target, lo in ((k_ref, D), (v_ref, 2 * D)):
                    part = row[:, lo + pair * 128 : lo + pair * 128 + 128]
                    target[c, pair, block, :] = jnp.where(mine, part, target[c, pair, block, :].astype(F32)).astype(BF)

        for store in stores():
            store.start()

    valid = lax.broadcasted_iota(jnp.int32, (1, KEYS - 128), 1) < JOINED - 128

    def mask(scores):
        return jnp.concatenate([scores[:, :128], jnp.where(valid, scores[:, 128:], -1e30)], axis=1)

    @pl.when(t >= videos_here)
    def _():
        first = i * frames_here

        @pl.loop(0, frames_here)
        def _(j):
            c = first + j
            for pair in range(PAIRS):

                def keep(head, p, pair=pair):
                    p_ref[j, pair, :, head * KEYS : head * KEYS + KEYS] = p

                out, inv = pair_fwd(q_ref[c, pair], k_ref[c, pair], v_ref[c, pair], mask, keep)
                inv_ref[j, pair] = inv
                mixed_ref[j, :, lanes(pair)] = out.astype(BF)

        attended = dims(mixed_ref[...].reshape(every, D), w_out1[...], 1, 0) + vec(out_bias1)
        kept_ref[...] = joined[pl.ds(first, frames_here)] + attended.reshape(frames_here, ROWS, D)

    @pl.when(t == 2 * videos_here - 1)
    def _():
        gather.finish()
        count = videos_here * FRAMES
        for video in range(video_size):
            unpack(video)
            cls_ref[video * count : video * count + count, :] = wide[...].astype(BF)
        for store in stores():
            store.wait()


def fc_parts(x, w, V):
    size, width = FF // UNITS // V, FF // UNITS
    return jnp.concatenate([x[:, q * width + w * size : q * width + w * size + size] for q in range(UNITS)], axis=1)


def proj_parts(x, w, V):
    size = D // V
    return jnp.concatenate([x[:, q * D + w * size : q * D + w * size + size] for q in range(4)], axis=1)


MLP_PARTS = (fc_parts, proj_parts)


def in_pieces(group, w, V):
    size, out = 3 * D // V, []
    for kind in range(3):
        first = kind * D + group * HALF
        lo, hi = max(first, w * size), min(first + HALF, w * size + size)
        if hi > lo:
            out.append((kind * HALF + lo - first, hi - lo, lo - w * size))
    return out


def in_width(V):
    return max(sum(piece[1] for piece in in_pieces(g, w, V)) for g in range(2) for w in range(V))


def attn_parts(group):
    def parts(x, w, V):
        pieces = [x[:, at : at + count] for at, count, _ in in_pieces(group, w, V)]
        short = in_width(V) - sum(piece.shape[1] for piece in pieces)
        if short:
            pieces.append(jnp.zeros((x.shape[0], short), F32))
        if group == 0:
            size = D // V
            pieces.append(x[:, 3 * HALF + w * size : 3 * HALF + w * size + size])
        return jnp.concatenate(pieces, axis=1) if len(pieces) > 1 else pieces[0]

    return parts


class Scatter:
    def __init__(self, place, step, acc, recv0, recv_bits, send3, recv3, result, sems, first=0):
        self.place, self.step, self.acc, self.first = place, step, acc, first
        self.recv0, self.recv_bits, self.send3, self.recv3, self.result = recv0, recv_bits, send3, recv3, result
        self.sems = sems
        self.n_bits = len(place.bits) - 1

    def other_core(self):
        return {"frame": self.place.f + 1 - 2 * self.place.core}

    def exchange0(self, unit, source):
        return remote(source, self.recv0.at[unit - self.first], self.sems["send0"].at[unit], self.sems["recv0"].at[unit], self.other_core())

    def order(self, core, stage):
        return stage if core == 0 else self.n_bits - 1 - stage

    def blocks(self, stage, flip):
        place, n = self.place, self.n_bits
        free = n - 1 - stage
        out = []
        for i in range(1 << free):
            both = []
            for core in range(2):
                done = [self.order(core, s) for s in range(stage)]
                now = self.order(core, stage)
                rest = [bit for bit in range(n) if bit not in done and bit != now]
                at = 0
                for bit in done:
                    at = at + place.bits[bit + 1] * (1 << bit)
                own = place.bits[now + 1]
                at = at + ((1 - own) if flip else own) * (1 << now)
                for index, bit in enumerate(rest):
                    at = at + ((i >> index) & 1) * (1 << bit)
                both.append(at)
            out.append((1 - place.core) * both[0] + place.core * both[1])
        return out

    def partner(self, stage):
        place = self.place
        moves = []
        for core in range(2):
            bit = self.order(core, stage) + 1
            moves.append((1 - 2 * place.bits[bit]) * (1 << bit))
        return {"frame": place.f + (1 - place.core) * moves[0] + place.core * moves[1]}

    def exchange(self, unit, stage, i, block):
        sems = self.sems
        return remote(
            self.acc(unit, block), self.recv_bits[stage].at[unit - self.first, i],
            sems["send_bits"].at[unit, stage, i], sems["recv_bits"].at[unit, stage, i], self.partner(stage),
        )

    def add(self, unit, block, came):
        target = self.acc(unit, block)
        target[...] = (target[...].astype(F32) + came.astype(F32)).astype(BF)

    def stage(self, unit, stage):
        if stage == 0:
            self.exchange0(unit, self.recv0.at[unit - self.first]).wait_recv()
            came = lambda position, block: self.recv0[unit - self.first, block]
        else:
            for i in range(1 << (self.n_bits - stage)):
                self.exchange(unit, stage - 1, i, 0).wait_recv()
            came = lambda position, block: self.recv_bits[stage - 1][unit - self.first, position]
        if stage == self.n_bits:
            block = self.own_block()
            self.add(unit, block, came(0, block))
            return
        sending, staying = self.blocks(stage, True), self.blocks(stage, False)
        where = self.positions(stage)
        for i, block in enumerate(sending):
            self.add(unit, block, came(where[1][i], block))
            self.exchange(unit, stage, i, block).start()
        for i, block in enumerate(staying):
            self.add(unit, block, came(where[0][i], block))

    def positions(self, stage):
        place, n = self.place, self.n_bits
        if stage == 0:
            return [[None] * (1 << (n - 1))] * 2
        out = [[], []]
        for flip in range(2):
            for i in range(1 << (n - 1 - stage)):
                both = []
                for core in range(2):
                    done = [self.order(core, s) for s in range(stage)]
                    now = self.order(core, stage)
                    rest_before = [bit for bit in range(n) if bit not in done]
                    rest = [bit for bit in rest_before if bit != now]
                    own = place.bits[now + 1]
                    at = 0
                    for index, bit in enumerate(rest_before):
                        if bit == now:
                            at = at + ((1 - own) if flip else own) * (1 << index)
                        else:
                            at = at + ((i >> rest.index(bit)) & 1) * (1 << index)
                    both.append(at)
                out[flip].append((1 - place.core) * both[0] + place.core * both[1])
        return out

    def own_block(self):
        return lax.div(self.place.f, 2)

    def across(self, unit, hop):
        place, sems = self.place, self.sems
        to = lax.rem(place.v + hop, place.V)
        return remote(
            self.send3.at[unit, to], self.recv3.at[unit, hop],
            sems["send3"].at[unit, hop], sems["recv3"].at[unit, hop], place.video_peer(hop),
        )

    def middle(self, unit):
        for stage in range(1, self.n_bits):
            self.stage(unit, stage)

    def land(self, unit):
        self.stage(unit, self.n_bits)
        return self.acc(unit, self.own_block())

    def send_video(self, unit, parts, value):
        value = value.astype(F32)
        for w in range(self.place.V):
            self.send3[unit, w] = parts(value, w, self.place.V).astype(BF)
        pl.loop(1, self.place.V)(lambda hop: self.across(unit, hop).start())

    def finish(self, unit):
        self.result[unit] = self.send3[unit, self.place.v].astype(F32)

        @pl.loop(1, self.place.V)
        def _(hop):
            self.across(unit, hop).wait_recv()
            self.result[unit] += self.recv3[unit, hop].astype(F32)

    def drain(self, unit, source):
        self.exchange0(unit, source).wait_send()
        for stage in range(self.n_bits):
            for i in range(1 << (self.n_bits - 1 - stage)):
                self.exchange(unit, stage, i, 0).wait_send()

    def drain_video(self, unit):
        pl.loop(1, self.place.V)(lambda hop: self.across(unit, hop).wait_send())


class Totals:
    def __init__(self, place, which, own, near, middle, far, result, sems):
        self.place, self.which, self.own, self.near_buf, self.middle = place, which, own, near, middle
        self.far_buf, self.result, self.sems = far, result, sems

    def near(self, step):
        sems = self.sems
        return remote(
            self.own, self.near_buf.at[self.which, step], sems["vec_send"].at[self.which, 0, step],
            sems["vec_recv"].at[self.which, 0, step], self.place.frame_peer(step),
        )

    def far(self, hop):
        sems = self.sems
        return remote(
            self.middle.at[self.which], self.far_buf.at[self.which, hop], sems["vec_send"].at[self.which, 1, hop],
            sems["vec_recv"].at[self.which, 1, hop], self.place.video_peer(hop),
        )

    def start(self):
        pl.loop(1, self.place.F)(lambda step: self.near(step).start())

    def forward(self):
        self.middle[self.which] = self.own[...]

        @pl.loop(1, self.place.F)
        def _(step):
            self.near(step).wait_recv()
            self.middle[self.which] += self.near_buf[self.which, step]

        pl.loop(1, self.place.V)(lambda hop: self.far(hop).start())

    def finish(self):
        self.result[self.which] = self.middle[self.which]

        @pl.loop(1, self.place.V)
        def _(hop):
            self.far(hop).wait_recv()
            self.result[self.which] += self.far_buf[self.which, hop]
            self.far(hop).wait_send()

        pl.loop(1, self.place.F)(lambda step: self.near(step).wait_send())


def mlp_kernel(
    frame_size, video_size, videos_here, frames_here,
    kept_ref, cot_ref, gain, shift, fc_bias, proj_bias, fc_hbm, proj_hbm,
    out_ref, grad_ref, done_ref, mid_ref, raw_hbm, sums,
    wide, normed2, cot2, act, grad_h, out_acc, grad_acc, bias_rows, bias_sums, fc_buf, proj_buf, fc_all,
    grads, recv0, recv_a, recv_b, recv_c, send3, recv3,
    s_load, s_raw, s_send0, s_recv0, s_sendb, s_recvb, s_send3, s_recv3,
):
    chunk = pl.program_id(0)
    frames = videos_here * frames_here
    place = Place(frame_size, video_size)
    step = D // frame_size // UNITS
    wide_step = 4 * step
    width = FF // UNITS
    sems = dict(send0=s_send0, recv0=s_recv0, send_bits=s_sendb, recv_bits=s_recvb, send3=s_send3, recv3=s_recv3)
    scatter = Scatter(
        place, step, lambda unit, block: grads.at[unit, 0, block], recv0, [recv_a, recv_b, recv_c], send3, recv3, done_ref, sems
    )
    sliced = wide_step % 128 == 0

    def rows_of(b, count=1):
        return pl.ds(pl.multiple_of(b * count * ROWS, ROWS), count * ROWS)

    def loads(c):
        slot = lax.rem(c, 2)
        out = []
        for f in range(frame_size):
            at = pl.multiple_of((f * UNITS + c) * wide_step, wide_step)
            to = slice(f * wide_step, f * wide_step + wide_step)
            out.append(pltpu.make_async_copy(proj_hbm.at[pl.ds(at, wide_step)], proj_buf.at[slot, to], s_load.at[slot, 0, f]))
            if sliced:
                out.append(pltpu.make_async_copy(fc_hbm.at[:, pl.ds(at, wide_step)], fc_buf.at[slot, :, to], s_load.at[slot, 1, f]))
        return out

    def load_all():
        return pltpu.make_async_copy(fc_hbm, fc_all, s_load.at[0, 1, 0])

    @pl.when(chunk == 0)
    def _():
        place.announce()
        for load in loads(chunk):
            load.start()
        if not sliced:
            load_all().start()
        sums[...] = jnp.zeros_like(sums)
        bias_sums[...] = jnp.zeros_like(bias_sums)
        wide[:, PATCHES:ROWS, :] = jnp.zeros((frames_here, ROWS - PATCHES, D), F32)
        bias = fc_bias[...].astype(F32).reshape(1, FF)
        for c in range(UNITS):
            for f in range(frame_size):
                at = (f * UNITS + c) * wide_step
                bias_rows[c : c + 1, f * wide_step : f * wide_step + wide_step] = bias[:, at : at + wide_step]

        @pl.loop(0, videos_here)
        def _(i):
            cot = cot_ref[i].astype(F32)
            for j in range(frames_here):
                wide[j, 0:PATCHES, :] = cot[:, j, :]
            for j in range(frames_here):
                b = i * frames_here + j
                cot_j = wide[j]
                cot2[rows_of(b), :] = cot_j.astype(BF)
                sums[6:7, :] += column_sum(cot_j)
                normed, _, _ = norm_fwd(kept_ref[b], vec(gain), vec(shift))
                normed2[rows_of(b), :] = normed.astype(BF)
                out_acc[rows_of(b), :] = kept_ref[b] + vec(proj_bias)
                grad_acc[rows_of(b), :] = jnp.zeros((ROWS, D), F32)

        if not sliced:
            load_all().wait()
        place.meet()

    for load in loads(chunk):
        load.wait()

    @pl.when(chunk < UNITS - 1)
    def _():
        for load in loads(chunk + 1):
            load.start()

    slot = lax.rem(chunk, 2)
    if not sliced:
        for c in range(UNITS):

            @pl.when(chunk == c)
            def _(c=c):
                for f in range(frame_size):
                    at = (f * UNITS + c) * wide_step
                    fc_buf[slot, :, f * wide_step : f * wide_step + wide_step] = fc_all[:, at : at + wide_step]

    fc, proj = fc_buf.at[slot], proj_buf.at[slot]
    bias = bias_rows[pl.ds(chunk, 1), :]
    per_tile = 2 if frames % 2 == 0 else 1
    tiles = frames // per_tile

    def due(c, t, now, call):
        pl.when(jnp.logical_and(chunk == c, now == min(t, tiles - 1)))(call)

    def both(call, first):
        return lambda: pl.loop(first, first + 2)(call)

    def video():
        for unit in range(2):
            scatter.send_video(unit, MLP_PARTS[unit % 2], scatter.land(unit)[...])

    @pl.loop(0, tiles)
    def _(t):
        due(1, 1, t, both(lambda unit: scatter.stage(unit, 0), 0))
        due(2, 0, t, both(scatter.middle, 0))
        due(2, 1, t, both(lambda unit: scatter.stage(unit, 0), 2))
        due(2, 2, t, video)
        rows = rows_of(t, per_tile)
        hidden = dims(normed2[rows, :], fc[...], 1, 0) + bias
        grad_a = dims(cot2[rows, :], proj[...], 1, 1)
        gate = 0.5 * jnp.tanh(0.851 * hidden) + 0.5
        active = hidden * gate
        grad = (grad_a * (gate + 1.702 * active * (1.0 - gate))).astype(BF)
        active = active.astype(BF)
        act[rows, :] = active
        grad_h[rows, :] = grad
        bias_sums[pl.ds(chunk, 1), :] += column_sum(grad.astype(F32))
        out_acc[rows, :] += dims(active, proj[...], 1, 0)
        grad_acc[rows, :] += dims(grad, fc[...], 1, 1)

    unit = 2 * chunk

    @pl.loop(0, 2)
    def _(m):
        size = width // 2
        count = frame_size // 4
        value = dims(act[:, pl.ds(pl.multiple_of(m * size, size), size)], cot2[...], 0, 0).astype(BF)
        value = value.reshape(count, 2, 4, step, D)
        for core in range(2):
            for q in range(4):
                grads[
                    unit + 1, lax.rem(core + place.core, 2), pl.ds(m * count, count), :, q * D : q * D + D
                ] = value[:, core, q]

    @pl.loop(0, 2)
    def _(m):
        size = D // 2
        value = dims(normed2[:, pl.ds(pl.multiple_of(m * size, size), size)], grad_h[...], 0, 0).astype(BF)
        count = frame_size // 4
        value = value.reshape(count, 2, UNITS, step, width)
        for core in range(2):
            for q in range(UNITS):
                grads[
                    unit, lax.rem(core + place.core, 2), pl.ds(m * count, count), :, q * width : q * width + width
                ] = value[:, core, q]

    def raw():
        return pltpu.make_async_copy(grads.at[pl.ds(4, 2)], raw_hbm, s_raw.at[0])

    def source(unit):
        return grads.at[unit, 1]

    @pl.when(chunk == 0)
    def _():
        pl.loop(0, 2)(lambda unit: scatter.exchange0(unit, source(unit)).start())

    @pl.when(chunk == 1)
    def _():
        pl.loop(2, 4)(lambda unit: scatter.exchange0(unit, source(unit)).start())

    @pl.when(chunk == 2)
    def _():
        raw().start()
        both(scatter.middle, 2)()
        both(scatter.finish, 0)()
        for c in range(UNITS):
            for f in range(frame_size):
                at = (f * UNITS + c) * wide_step
                row, column = 2 + at // D, at % D
                sums[row : row + 1, column : column + wide_step] = bias_sums[
                    c : c + 1, f * wide_step : f * wide_step + wide_step
                ]

        @pl.loop(0, videos_here)
        def _(i):
            outs = [out_acc[rows_of(i * frames_here + j), :][:PATCHES] for j in range(frames_here)]
            out_ref[i] = jnp.stack(outs, axis=1).astype(BF)

        @pl.loop(0, frames)
        def _(b):
            rows = rows_of(b)
            _, unit, inv = norm_fwd(kept_ref[b], vec(gain), vec(shift))
            grad = grad_acc[rows, :]
            sums[0:1, :] += column_sum(grad * unit)
            sums[1:2, :] += column_sum(grad)
            grad_ref[b] = norm_back(grad, unit, inv, vec(gain)) + cot2[rows, :].astype(F32)

        @pl.loop(0, 2)
        def _(unit):
            mid_ref[unit] = scatter.land(2 + unit)[...]
            scatter.drain_video(unit)

        pl.loop(0, 4)(lambda unit: scatter.drain(unit, source(unit)))
        raw().wait()


def attn_back_kernel(
    frame_size, video_size, videos_here, frames_here,
    x_hbm, normed_hbm, w_in_hbm, msg_ref, gk_ref, gain, shift, w_out, mlp_sums, mid_ref, raw_hbm, cls_ref, *rest,
):
    msg_operands, rest = rest[:8], rest[8:]
    (
        mixed_ref, q_ref, k_ref, v_ref, p_ref, inv_ref,
        tg_ref, reduced_ref, near_ref, far_ref, totals_ref, msg_ref_out, in_ref_out, out_ref_out, msg_sums, grad_cls,
        x_ref, normed_ref, w_in, joined, staged, gqkv_all, gk_all, sums, gm_grads, gm_wide, gm_own, gm_rows, gm_all, wide, cls_grads,
        acc_mlp, *rest,
    ) = rest
    last_buffers, rest = rest[:6], rest[6:]
    (acc_near, *near_buffers), rest = rest[:7], rest[7:]
    (acc_far, *far_buffers), rest = rest[:7], rest[7:]
    (vec_near, vec_mid, vec_far), rest = rest[:3], rest[3:]
    msg_kept, (msg_gqkv, msg_mixed), msg_state, rest = list(rest[:7]), rest[7:9], rest[9:15], rest[15:]
    msg_kept.insert(6, gqkv_all.at[0:D])
    (s_late, s_msg, s_local, s_staged, s_vsend, s_vrecv, s_gsend, s_grecv), rest = rest[:8], rest[8:]
    names = ("send0", "recv0", "send_bits", "recv_bits", "send3", "recv3")
    last_sems, near_sems, far_sems = (dict(zip(names, rest[6 * i : 6 * i + 6])) for i in range(3))
    frames = videos_here * frames_here
    steps = 2 * frames
    t = pl.program_id(0)
    side, b = lax.div(t, frames), lax.rem(t, frames)
    place = Place(frame_size, video_size)
    step = D // frame_size // UNITS
    total = frames * ROWS
    each_mid, each_last, each_attn = pl.loop(0, 2), pl.loop(2, 4), pl.loop(0, UNITS)

    def scatter(acc, buffers, result, sems, first=0):
        recv0, recv_a, recv_b, recv_c, send3, recv3 = buffers
        return Scatter(place, step, acc, recv0, [recv_a, recv_b, recv_c], send3, recv3, result, sems, first)

    lasts = scatter(lambda unit, block: acc_mlp.at[unit - 2, block], last_buffers, reduced_ref, last_sems, first=2)
    near = scatter(lambda unit, block: acc_near.at[0, unit, block], near_buffers, near_ref, near_sems)
    far = scatter(lambda unit, block: acc_far.at[0, unit, block], far_buffers, far_ref, far_sems)
    vec_sems = dict(vec_send=s_vsend, vec_recv=s_vrecv)
    early = Totals(place, 0, mlp_sums, vec_near, vec_mid, vec_far, totals_ref, vec_sems)
    late = Totals(place, 1, sums, vec_near, vec_mid, vec_far, totals_ref, vec_sems)
    gather = Gather(place, gm_own, gm_rows, s_gsend, s_grecv)

    def last_source(unit):
        return raw_hbm.at[unit - 2, 1]

    def local(unit):
        return pltpu.make_async_copy(raw_hbm.at[unit - 2, 0], acc_mlp.at[unit - 2], s_local.at[unit - 2])

    def msg_loads():
        return [pltpu.make_async_copy(a, b, s_msg.at[i]) for i, (a, b) in enumerate(zip(msg_operands, msg_kept))]

    def late_loads():
        out = [
            pltpu.make_async_copy(x_hbm, x_ref, s_late.at[0]), pltpu.make_async_copy(normed_hbm, normed_ref, s_late.at[1]),
        ]
        for half_at in range(2):
            for kind in range(3):
                source = w_in_hbm.at[:, kind * D + half_at * HALF : kind * D + half_at * HALF + HALF]
                at = (half_at * 3 + kind) * HALF
                out.append(pltpu.make_async_copy(source, w_in.at[:, at : at + HALF], s_late.at[2 + half_at * 3 + kind]))
        return out

    def due(at, call):
        pl.when(t == min(at, steps - 1))(call)

    def begin():
        place.greet()
        sums[...] = jnp.zeros_like(sums)

        @each_last
        def _(unit):
            lasts.exchange0(unit, last_source(unit)).start()
            local(unit).start()

        early.start()
        for load in late_loads():
            load.start()
        for at, load in enumerate(msg_loads()):
            if at != 6:
                load.start()
        for unit in range(2):
            lasts.send_video(unit, MLP_PARTS[unit], mid_ref[unit])

    def open_lasts():
        @each_last
        def _(unit):
            local(unit).wait()
            lasts.stage(unit, 0)

    def land_lasts():
        for unit in (2, 3):
            lasts.send_video(unit, MLP_PARTS[unit % 2], lasts.land(unit)[...])

    def land(scatter, group):
        @each_attn
        def _(unit):
            scatter.send_video(unit, attn_parts(group), scatter.land(unit)[...])

    due(0, begin)
    due(2, open_lasts)
    due(4, lambda: each_mid(lasts.finish))
    due(5, early.forward)
    due(6, lambda: each_last(lasts.middle))
    due(8, land_lasts)
    due(frames + 2, lambda: each_attn(lambda unit: near.stage(unit, 0)))
    due(steps - 1, lambda: each_last(lasts.finish))
    rows = pl.ds(pl.multiple_of(b * ROWS, ROWS), ROWS)
    side_lanes = pl.ds(pl.multiple_of(side * HALF, HALF), HALF)

    @pl.when(side == 0)
    def _():
        gk_low = gk_ref[b].astype(BF)
        gk_all[b] = gk_low
        sums[0:1, :] += column_sum(gk_low.astype(F32))

    grad_mixed = dims(gk_all[b], w_out[side_lanes, :], 1, 1)
    for pair in range(PAIRS // 2):
        grads = pair_back(
            q_ref[0, pair], k_ref[0, pair], v_ref[0, pair], grad_mixed[:, lanes(pair)],
            mixed_ref[b, :, pl.ds(pl.multiple_of(side * HALF + pair * 128, 128), 128)], inv_ref[0, pair],
            lambda head, pair=pair: p_ref[0, pair, :, head * KEYS : head * KEYS + KEYS],
        )
        for kind in range(3):
            at = pl.ds(pl.multiple_of((side * 3 + kind) * HALF + pair * 128, 128), 128)
            gqkv_all[rows, at] = grads[kind][:ROWS].astype(BF)
    for row, kind in ((1, 0), (2, 2)):
        part = gqkv_all[rows, pl.ds(pl.multiple_of((side * 3 + kind) * HALF, HALF), HALF)]
        sums[row : row + 1, side_lanes] += column_sum(part.astype(F32))

    def attn_unit(m, target, left, right, lo):
        size, width = D // 2, right.shape[1]
        value = dims(left[:, :, pl.ds(pl.multiple_of(m * size, size), size)].reshape(total, size), right, 0, 0).astype(BF)
        count = frame_size // 4
        value = value.reshape(count, 2, UNITS, step, width)
        for u in range(UNITS):
            for core in range(2):
                target[lax.rem(core + place.core, 2), u, pl.ds(m * count, count), :, lo : lo + width] = value[:, core, u]

    def attn_units(group, target, scatter):
        @pl.loop(0, 2)
        def _(m):
            attn_unit(m, target, normed_ref, gqkv_all[0:total, group * 3 * HALF : (group + 1) * 3 * HALF], 0)
            if group == 0:
                attn_unit(m, target, mixed_ref, gk_all[...].reshape(total, D), 3 * HALF)

        each_attn(lambda unit: scatter.exchange0(unit, target.at[1, unit]).start())

    @pl.when(t == frames - 1)
    def _():
        for load in late_loads():
            load.wait()
        attn_units(0, acc_near, near)

    @pl.when(t == steps - 1)
    def _():
        at = JOINED - 1 - (JOINED - 1) % 16
        gm_grads[...] = jnp.zeros_like(gm_grads)
        for c in range(frames):
            piece = gqkv_all[c * ROWS + at : c * ROWS + at + 16, :].astype(F32)
            gm_grads[c : c + 1, :] = piece[PATCHES - at : PATCHES - at + 1]
            joined[c : c + 1, :] = msg_ref[c]
        _, unit, inv = norm_fwd(joined[0:frames, :], vec(gain), vec(shift))
        grad = dims(gm_grads[...].astype(BF), w_in[...], 1, 1)[0:frames]
        gm_wide[0:frames, :] = norm_back(grad, unit, inv, vec(gain))
        for i in range(videos_here):
            gm_own[i] = gm_wide[i * frames_here : i * frames_here + frames_here, :].astype(BF)
            gm_rows[place.v, i, place.f] = gm_own[i]
        gather.start()
        each_attn(near.middle)
        attn_units(1, acc_far, far)
        early.finish()
        gather.near()
        gather.forward()

        def put(i, j):
            return pltpu.make_async_copy(staged.at[j], tg_ref.at[i, :, j], s_staged.at[j])

        def norm_frames(lo, hi):
            @pl.loop(lo, hi)
            def _(i):
                x = x_ref[i].astype(F32)
                for j in range(frames_here):
                    c = i * frames_here + j
                    joined[0:PATCHES, :] = x[:, j, :]
                    joined[PATCHES:ROWS, :] = jnp.zeros((ROWS - PATCHES, D), F32)
                    joined[PATCHES : PATCHES + 1, :] = msg_ref[c]
                    _, unit, inv = norm_fwd(joined[...], vec(gain), vec(shift))
                    rows = pl.ds(pl.multiple_of(c * ROWS, ROWS), ROWS)
                    grad = dims(gqkv_all[rows, :], w_in[...], 1, 1)
                    sums[3:4, :] += column_sum(grad * unit)
                    sums[4:5, :] += column_sum(grad)
                    pl.when(i > 0)(lambda j=j: put(i - 1, j).wait())
                    staged[j] = (gk_ref[c] + norm_back(grad, unit, inv, vec(gain)))[:PATCHES]
                    put(i, j).start()

        norm_frames(0, 1)
        each_attn(lambda unit: far.stage(unit, 0))
        land(near, 0)
        norm_frames(1, videos_here)
        msg_loads()[6].start()
        late.start()
        each_attn(far.middle)
        each_attn(near.finish)
        for load in msg_loads():
            load.wait()
        for ref in (msg_sums, msg_ref_out, in_ref_out, out_ref_out):
            ref[...] = jnp.zeros_like(ref)
        count = videos_here * FRAMES

        def between():
            land(far, 1)
            late.forward()
            gather.finish()
            for video in range(video_size):
                for i in range(videos_here):
                    for f in range(frame_size):
                        at_row = (i * frame_size + f) * frames_here
                        wide[at_row : at_row + frames_here, :] = gm_rows[video, i, f].astype(F32)
                gm_all[video * count : video * count + count, :] = wide[...].astype(BF)

        blocks = video_size * count // BLOCK
        if blocks > 1:
            between()

        @pl.loop(0, blocks)
        def _(block):
            at = pl.ds(pl.multiple_of(block * BLOCK, BLOCK), BLOCK)
            msg_back_block(
                place, cls_ref[at, :], gm_all.at[at], msg_kept, msg_ref_out, in_ref_out, out_ref_out, msg_sums, cls_grads.at[at],
                msg_state, msg_gqkv, msg_mixed, between if blocks == 1 else lambda: None,
            )

        for i in range(videos_here):
            for j in range(frames_here):
                row = (place.v * videos_here + i) * FRAMES + place.f * frames_here + j
                grad_cls[i * frames_here + j] = cls_grads[pl.ds(row, 1), :]
        for j in range(frames_here):
            put(videos_here - 1, j).wait()
        late.finish()
        each_attn(far.finish)
        each_last(lambda unit: lasts.drain(unit, last_source(unit)))
        pl.loop(0, 4)(lasts.drain_video)

        @each_attn
        def _(unit):
            for scatter, target in ((near, acc_near), (far, acc_far)):
                scatter.drain(unit, target.at[1, unit])
                scatter.drain_video(unit)


def msg_back_block(place, cls, gm_ref, kept, acc_msg, acc_in, acc_out, sums, cls_grad, scratch, gqkv, grad_mixed, between):
    bias, gain, shift, in_bias, out_bias, w_msg, w_in, w_out = kept
    qkv, probs, invs, mixed, normed, _ = scratch
    own_rows = D // place.F
    padded = acc_msg.shape[0]

    def own_columns(x):
        return pltpu.roll(x.astype(F32), lax.rem(D - place.f * own_rows, D), 1)[:, :padded].astype(BF)

    unit, inv_std = msg_forward(cls, (bias, gain, shift, in_bias, out_bias), w_msg, w_in, w_out, scratch, PAIRS // 2)
    between()
    gm = gm_ref[...]
    acc_out[...] += dims(own_columns(mixed[...]), gm, 0, 0)
    sums[5:6, :] += column_sum(gm.astype(F32))
    grad_mixed[...] = dims(gm, w_out[...], 1, 1)

    @pl.loop(0, PAIRS, unroll=PAIRS // 2)
    def _(pair):
        at = pair_lanes(pair)
        grads = pair_back(
            qkv[:, at], qkv[:, pair_lanes(pair, 1)], qkv[:, pair_lanes(pair, 2)], grad_mixed[:, at],
            mixed[:, at], invs[:, at], lambda head: probs[2 * pair + head],
        )
        for kind in range(3):
            gqkv[:, pair_lanes(pair, kind)] = grads[kind].astype(BF)

    own_normed = own_columns(normed[...])
    grad = None
    for kind in range(3):
        columns = slice(kind * D, kind * D + D)
        part = gqkv[:, columns]
        acc_in[:, columns] += dims(own_normed, part, 0, 0)
        if kind != 1:
            row = 3 + kind // 2
            sums[row : row + 1, :] += column_sum(part.astype(F32))
        term = dims(part, w_in[:, columns], 1, 1)
        grad = term if grad is None else grad + term
    sums[1:2, :] += column_sum(grad * unit)
    sums[2:3, :] += column_sum(grad)
    grad_message = norm_back(grad, unit, inv_std, vec(gain)) + gm.astype(F32)
    grad_message = grad_message.astype(BF)
    acc_msg[...] += dims(own_columns(cls), grad_message, 0, 0)
    sums[0:1, :] += column_sum(grad_message.astype(F32))
    cls_grad[...] = dims(grad_message, w_msg[...], 1, 1)


def collect_kernel(
    frame_size, video_size, videos_here, frames_here,
    done, reduced, near, far, totals, acc_msg, acc_in, acc_out, sums, grad_cls, tg_hbm, output_hbm,
    output, tokens_grad, msg_grad, in_grad, out_grad, *rest,
):
    (
        msg_bias_g, msg_gain_g, msg_shift_g, msg_in_bias_g, msg_out_bias_g, gain1_g, shift1_g,
        attn_in_g, attn_in_bias_g, attn_out_g, attn_out_bias_g, gain2_g, shift2_g, fc_g, fc_bias_g, proj_g, proj_bias_g,
        tg, out, sem,
    ) = rest
    f, v = lax.axis_index("frame"), lax.axis_index("video")
    own_rows = D // frame_size

    def load(i):
        return pltpu.make_async_copy(tg_hbm.at[i], tg.at[i], sem.at[0, i])

    def store(i):
        return pltpu.make_async_copy(tg.at[i], tokens_grad.at[i], sem.at[0, i])

    def load_out(i):
        return pltpu.make_async_copy(output_hbm.at[i], out.at[i], sem.at[1, i])

    def store_out(i):
        return pltpu.make_async_copy(out.at[i], output.at[i], sem.at[1, i])

    for i in range(videos_here):
        load(i).start()
        load_out(i).start()
    for i in range(videos_here):
        load(i).wait()
        added = [grad_cls[i * frames_here + j] for j in range(frames_here)]
        tg[i, 0] = tg[i, 0] + jnp.concatenate(added, axis=0)
        store(i).start()
        load_out(i).wait()
        store_out(i).start()

    def own_matrix(target, x):
        size = x.shape[1] // video_size
        target[...] = pltpu.roll(x[:own_rows], lax.rem(x.shape[1] - v * size, x.shape[1]), 1)[:, :size]

    own_matrix(msg_grad, acc_msg[...])
    own_matrix(in_grad, acc_in[...])
    own_matrix(out_grad, acc_out[...])

    def own_vector(target, ref, first, count):
        size = count * D // frame_size
        per_row = frame_size // count
        row = first + lax.div(f, per_row)
        x = ref[pl.ds(row, 1), :]
        x = pltpu.roll(jnp.broadcast_to(x, (8, D)), lax.rem(D - lax.rem(f, per_row) * size, D), 1)
        target[...] = x[0:1, :size].reshape(size)

    mlp_sums, attn_sums = totals.at[0], totals.at[1]
    for target, ref, first, count in (
        (msg_bias_g, sums, 0, 1), (msg_gain_g, sums, 1, 1), (msg_shift_g, sums, 2, 1), (msg_in_bias_g, sums, 3, 2),
        (msg_out_bias_g, sums, 5, 1), (gain1_g, attn_sums, 3, 1), (shift1_g, attn_sums, 4, 1),
        (attn_in_bias_g, attn_sums, 1, 2), (attn_out_bias_g, attn_sums, 0, 1), (gain2_g, mlp_sums, 0, 1),
        (shift2_g, mlp_sums, 1, 1), (fc_bias_g, mlp_sums, 2, 4), (proj_bias_g, mlp_sums, 6, 1),
    ):
        own_vector(target, ref, first, count)
    step = own_rows // UNITS
    columns = D // video_size
    wide_step = 4 * step
    part = FF // UNITS // video_size
    fc = [done[0], reduced[0], reduced[2]]
    for c in range(UNITS):
        for q in range(UNITS):
            for g in range(frame_size // video_size):
                from_at = q * part + g * wide_step
                to = (g * UNITS + c) * wide_step
                fc_g[q * step : q * step + step, to : to + wide_step] = fc[c][:, from_at : from_at + wide_step]
    for u in range(UNITS):
        rows = slice(u * step, u * step + step)
        attn_out_g[rows, :] = near[u][:, in_width(video_size) :]
        for w in range(video_size):

            @pl.when(v == w)
            def _(rows=rows, u=u, w=w):
                for group, parts in enumerate((near, far)):
                    at = 0
                    for _, count, to in in_pieces(group, w, video_size):
                        attn_in_g[rows, to : to + count] = parts[u][:, at : at + count]
                        at += count

    proj = [done[1], reduced[1], reduced[3]]
    proj = [x[:, q * columns : q * columns + columns] for x in proj for q in range(4)]
    proj_g[...] = jnp.concatenate(proj, axis=0).T
    for i in range(videos_here):
        store(i).wait()
        store_out(i).wait()


def shaped(shape, dtype):
    return jax.ShapeDtypeStruct(shape, dtype)


def whole(array):
    shape = array.shape
    return pl.BlockSpec(shape, lambda *_: (0,) * len(shape), pipeline_mode=pl.Buffered(1))


def wholes(*arrays):
    return [whole(array) for array in arrays]


def in_hbm():
    return pl.BlockSpec(memory_space=pl.ANY)


def in_vmem():
    return pl.BlockSpec(memory_space=pltpu.VMEM)


def per_step(count, shape):
    return pl.BlockSpec((count,) + shape, lambda b: (b,) + (0,) * len(shape))


def params(mib, **more):
    return pltpu.CompilerParams(vmem_limit_bytes=mib * MIB, **more)


def on_device(frame_size, video_size, *args):
    (
        tokens, cotangent, msg_weight, msg_bias, msg_norm_gain, msg_norm_shift, msg_in_weight,
        msg_in_bias, msg_out_weight, msg_out_bias, norm1_gain, norm1_shift, attn_in_weight,
        attn_in_bias, attn_out_weight, attn_out_bias, norm2_gain, norm2_shift, fc_weight, fc_bias,
        proj_weight, proj_bias,
    ) = args
    videos_here, frames_here = tokens.shape[:2]
    frames = videos_here * frames_here
    msgs = videos_here * video_size * FRAMES
    group = videos_here * FRAMES
    total = frames * ROWS
    F, V = frame_size, video_size
    step = D // F // UNITS
    n_bits = int(math.log2(F)) - 1
    x = tokens.transpose(0, 2, 1, 3)
    cot = cotangent.transpose(0, 2, 1, 3)
    msg_vectors = (msg_bias, msg_norm_gain, msg_norm_shift, msg_in_bias, msg_out_bias)
    DMA = pltpu.SemaphoreType.DMA

    msg_arrays = (*msg_vectors, msg_weight, msg_in_weight, msg_out_weight)
    kv_shape = (frames, PAIRS, KEYS, 128)

    def second(shape):
        zeros = (0,) * len(shape)
        return pl.BlockSpec((frames_here,) + shape, lambda t: (jnp.maximum(t - videos_here, 0),) + zeros)

    block_shapes = [(PAIRS, ROWS, 2 * KEYS), (PAIRS, ROWS, 128), (ROWS, D), (ROWS, D)]
    fwd_outs = [
        shaped((frames, PAIRS, ROWS, 128), BF), shaped(kv_shape, BF), shaped(kv_shape, BF), shaped((frames, ROWS, D), BF),
        shaped((frames,) + block_shapes[0], BF), shaped((frames,) + block_shapes[1], F32),
        shaped((frames,) + block_shapes[2], BF), shaped((frames,) + block_shapes[3], F32),
        shaped((frames, 1, D), F32), shaped((msgs, D), BF),
    ]
    q, k, v, normed, p, inv, mixed, kept, msg_out, cls = pl.pallas_call(
        functools.partial(attn_fwd_kernel, F, V, frames_here, videos_here),
        grid=(2 * videos_here,),
        in_specs=[
            pl.BlockSpec((1, PATCHES, frames_here, D), lambda t: (jnp.minimum(t, videos_here - 1), 0, 0, 0)), in_hbm(),
        ]
        + wholes(norm1_gain, norm1_shift, attn_in_bias, attn_out_bias, attn_in_weight) + [in_hbm()] * 9,
        out_specs=[in_hbm()] * 4 + [second(shape) for shape in block_shapes] + wholes(*fwd_outs[8:]),
        out_shape=fwd_outs,
        scratch_shapes=[pltpu.VMEM(out.shape, BF) for out in fwd_outs[:4]]
        + [
            pltpu.VMEM((frames, ROWS, D), F32), pltpu.VMEM((D, D), BF),
            pltpu.VMEM((16, D), F32), pltpu.VMEM((16, 3 * D), F32),
            pltpu.VMEM((videos_here, frames_here, D), BF),
            pltpu.VMEM((V, videos_here, F, frames_here, D), BF),
            pltpu.VMEM((group, D), F32), pltpu.VMEM((group, D), F32),
        ]
        + [pltpu.VMEM(a.shape, BF) for a in msg_arrays]
        + msg_scratch(group) + [DMA((V, F + V)), DMA((V, F + V)), DMA((11,)), DMA((4,))],
        compiler_params=params(63, collective_id=1, has_side_effects=True),
        name="attn_fwd",
    )(x, x, norm1_gain, norm1_shift, attn_in_bias, attn_out_bias, attn_in_weight, attn_out_weight, *msg_arrays)

    def bit_buffers(units, width=FF):
        return [
            pltpu.VMEM((units, max(1, F >> (2 + i)), step, width), BF) if i < n_bits else pltpu.VMEM((1, 1, 16, 128), BF)
            for i in range(3)
        ]

    def exchange_sems(units):
        return [DMA((units,)), DMA((units,)), DMA((units, n_bits, F // 4)), DMA((units, n_bits, F // 4)), DMA((units, V)), DMA((units, V))]

    def unit_buffers(count, units):
        return [pltpu.VMEM((count,) + shape, BF) for shape in units]

    block_shape = (F // 2, step, FF)
    part_shape = (V, step, FF // V)
    width = FF // UNITS
    mlp_outs = [
        shaped(x.shape, BF), shaped(kept.shape, F32), shaped((2, step, FF // V), F32), shaped((2, step, FF), BF),
        shaped((2, 2) + block_shape, BF), shaped((8, D), F32),
    ]
    output, grad_kept, done, mid, raw, mlp_sums = pl.pallas_call(
        functools.partial(mlp_kernel, F, V, videos_here, frames_here),
        grid=(UNITS,),
        in_specs=wholes(kept, cot, norm2_gain, norm2_shift, fc_bias, proj_bias) + [in_hbm(), in_hbm()],
        out_specs=wholes(*mlp_outs[:4]) + [in_hbm()] + wholes(mlp_outs[5]),
        out_shape=mlp_outs,
        scratch_shapes=[
            pltpu.VMEM((frames_here, ROWS, D), F32),
            pltpu.VMEM((total, D), BF), pltpu.VMEM((total, D), BF), pltpu.VMEM((total, width), BF), pltpu.VMEM((total, width), BF),
            pltpu.VMEM((total, D), F32), pltpu.VMEM((total, D), F32),
            pltpu.VMEM((UNITS, width), F32), pltpu.VMEM((UNITS, width), F32),
            pltpu.VMEM((2, D, width), BF), pltpu.VMEM((2, width, D), BF),
            pltpu.VMEM((D, FF) if 4 * step % 128 else (16, 128), BF),
            pltpu.VMEM((2 * UNITS, 2) + block_shape, BF), pltpu.VMEM((4,) + block_shape, BF),
        ]
        + bit_buffers(4) + unit_buffers(2, [part_shape] * 2)
        + [DMA((2, 2, F)), DMA((1,))] + exchange_sems(4),
        compiler_params=params(63, collective_id=2, has_side_effects=True),
        name="mlp",
    )(kept, cot, norm2_gain, norm2_shift, fc_bias, proj_bias, fc_weight, proj_weight)

    rows_own, columns = D // F, D // V
    padded = -(-rows_own // 128) * 128
    widths = (3 * HALF + D, 3 * HALF)
    part_widths = (in_width(V) + columns, in_width(V))
    back_outs = [
        shaped(x.shape, F32), shaped((4, step, FF // V), F32), shaped((UNITS, step, part_widths[0]), F32),
        shaped((UNITS, step, part_widths[1]), F32), shaped((2, 8, D), F32),
        shaped((padded, D), F32), shaped((padded, 3 * D), F32), shaped((padded, D), F32), shaped((8, D), F32),
        shaped((frames, 1, D), F32),
    ]
    def group_buffers(width, part_width):
        block = (F // 2, step, width)
        return [pltpu.VMEM((2, UNITS) + block, BF), pltpu.VMEM((UNITS,) + block, BF)] + bit_buffers(UNITS, width) + [
            pltpu.VMEM((UNITS, V, step, part_width), BF)
        ] * 2

    def by_pairs(shape):
        return pl.BlockSpec((1, PAIRS // 2) + shape, lambda t: (lax.rem(t, frames), lax.div(t, frames), 0, 0))

    tg, reduced, near, far, totals, acc_msg, acc_in, acc_out, msg_sums, grad_cls = pl.pallas_call(
        functools.partial(attn_back_kernel, F, V, videos_here, frames_here),
        grid=(2 * frames,),
        in_specs=[in_hbm()] * 3
        + wholes(msg_out, grad_kept, norm1_gain, norm1_shift, attn_out_weight, mlp_sums, mid)
        + [in_hbm()] + wholes(cls) + [in_hbm()] * 8 + wholes(mixed)
        + [by_pairs(shape) for shape in ((ROWS, 128), (KEYS, 128), (KEYS, 128), (ROWS, 2 * KEYS), (ROWS, 128))],
        out_specs=[in_hbm()] + wholes(*back_outs[1:]),
        out_shape=back_outs,
        scratch_shapes=[
            pltpu.VMEM(x.shape, BF), pltpu.VMEM(normed.shape, BF), pltpu.VMEM((D, 3 * D), BF),
            pltpu.VMEM((ROWS, D), F32), pltpu.VMEM((frames_here, PATCHES, D), F32),
            pltpu.VMEM((max(total, D), 3 * D), BF), pltpu.VMEM((frames, ROWS, D), BF), pltpu.VMEM((8, D), F32), pltpu.VMEM((16, 3 * D), F32), pltpu.VMEM((8, D), F32),
            pltpu.VMEM((videos_here, frames_here, D), BF), pltpu.VMEM((V, videos_here, F, frames_here, D), BF),
            pltpu.VMEM((msgs, D), BF), pltpu.VMEM((group, D), F32), pltpu.VMEM((msgs, D), F32),
            pltpu.VMEM((2,) + block_shape, BF), pltpu.VMEM((2,) + block_shape, BF),
        ]
        + bit_buffers(2) + unit_buffers(4, [part_shape] * 2)
        + group_buffers(widths[0], part_widths[0]) + group_buffers(widths[1], part_widths[1])
        + [pltpu.VMEM((2, F, 8, D), F32), pltpu.VMEM((2, 8, D), F32), pltpu.VMEM((2, V, 8, D), F32)]
        + [pltpu.VMEM(a.shape, BF) for a in msg_arrays if a is not msg_in_weight]
        + [pltpu.VMEM((BLOCK, 3 * D), BF), pltpu.VMEM((BLOCK, D), F32)] + msg_scratch(BLOCK)
        + [DMA((8,)), DMA((8,)), DMA((2,)), DMA((frames_here,))]
        + [DMA((2, 2, max(F, V))), DMA((2, 2, max(F, V))), DMA((V, F + V)), DMA((V, F + V))]
        + exchange_sems(4) + exchange_sems(UNITS) + exchange_sems(UNITS),
        compiler_params=params(63, collective_id=3, has_side_effects=True),
        name="attn_back",
    )(
        x, normed, attn_in_weight, msg_out, grad_kept, norm1_gain, norm1_shift, attn_out_weight, mlp_sums, mid, raw, cls,
        *msg_arrays, mixed, q, k, v, p, inv,
    )

    out_shapes = [
        (rows_own, columns), (rows_own, 3 * columns), (rows_own, columns),
        (rows_own,), (rows_own,), (rows_own,), (2 * rows_own,), (rows_own,), (rows_own,), (rows_own,),
        (rows_own, 3 * columns), (2 * rows_own,), (rows_own, columns), (rows_own,), (rows_own,), (rows_own,),
        (rows_own, 4 * columns), (4 * rows_own,), (columns, 4 * rows_own), (rows_own,),
    ]
    out_shapes = [shaped(shape, F32) for shape in out_shapes]
    (
        output, tokens_grad, msg_grad, msg_in_grad, msg_out_grad,
        msg_bias_g, msg_gain_g, msg_shift_g, msg_in_bias_g, msg_out_bias_g, gain1_g, shift1_g,
        attn_in_g, attn_in_bias_g, attn_out_g, attn_out_bias_g, gain2_g, shift2_g, fc_g, fc_bias_g, proj_g, proj_bias_g,
    ) = pl.pallas_call(
        functools.partial(collect_kernel, F, V, videos_here, frames_here),
        grid=(1,),
        in_specs=wholes(done, reduced, near, far, totals, acc_msg, acc_in, acc_out, msg_sums, grad_cls) + [in_hbm()] * 2,
        out_specs=[in_hbm()] * 2 + wholes(*out_shapes),
        out_shape=[shaped(x.shape, BF), shaped(x.shape, F32)] + out_shapes,
        scratch_shapes=[pltpu.VMEM(x.shape, F32), pltpu.VMEM(x.shape, BF), DMA((2, videos_here))],
        compiler_params=params(63),
        name="collect",
    )(done, reduced, near, far, totals, acc_msg, acc_in, acc_out, msg_sums, grad_cls, tg, output)

    return (
        output.transpose(0, 2, 1, 3), tokens_grad.transpose(0, 2, 1, 3),
        msg_grad, msg_bias_g, msg_gain_g, msg_shift_g, msg_in_grad, msg_in_bias_g, msg_out_grad, msg_out_bias_g,
        gain1_g, shift1_g, attn_in_g, attn_in_bias_g, attn_out_g, attn_out_bias_g,
        gain2_g, shift2_g, fc_g, fc_bias_g, proj_g.T, proj_bias_g,
    )


def solution(mesh):
    rows = P("video", "frame", None, None)
    matrix, vector = P("frame", "video"), P("frame")
    out_specs = (
        rows, rows,
        matrix, vector, vector, vector, matrix, vector, matrix, vector,
        vector, vector, matrix, vector, matrix, vector,
        vector, vector, matrix, vector, matrix, vector,
    )
    return jax.shard_map(
        functools.partial(on_device, mesh.shape["frame"], mesh.shape["video"]),
        mesh=mesh, in_specs=(rows, rows) + (P(),) * 20, out_specs=out_specs, check_vma=False,
    )
```

profile of v0, /device:TPU:0, one launch (start us, length us, event | category | flops | bytes accessed | tf_op | source)
XLA Modules:
  0.0 183.9 jit_solution(16204125225549716497)
XLA Ops:
  0.7 30.1 %attn_fwd.1 = (bf16[6,6,208,128]{3,2,1,0:T(8,128)(2,1)}, bf16[6,6,256,128]{3,2,1,0:T(8,128)(2,1)}, bf16[6,6,256,128]{3,2,1,0:T(8,128)(2,1)}, bf16[6,208,768]{2,1...) custom-call(bf16[3,197,2,768]{3,2,1,0:T(2,128)(2,1)} %bitcast.5, ...), custom_call_target="tpu_custom_call" | custom-call | tf_op jit(solution)/shard_map/attn_fwd/pallas_call | solution.py:1268
  30.8 63.5 %mlp.1 = (bf16[3,197,2,768]{3,2,1,0:T(2,128)(2,1)}, f32[6,208,768]{2,1,0:T(8,128)}, f32[2,32,768]{2,1,0:T(8,128)}, bf16[2,32,3072]{2,1,0:T(8,128)(2,1)}, bf16[2,...) custom-call(f32[6,208,768]{2,1,0:T(8,128)} %get-tuple-element.70.kept_ref, bf16[3,197,2,768]{3,2,1,0:T(2,128)(2,1)} %bitcast.8, ...), custom_call_target="tpu_custom_call" | custom-call | tf_op jit(solution)/shard_map/mlp/pallas_call | solution.py:1310
  94.3 81.7 %attn_back.1 = (f32[3,197,2,768]{3,2,1,0:T(2,128)}, f32[4,32,768]{2,1,0:T(8,128)}, f32[3,32,576]{2,1,0:T(8,128)}, f32[3,32,384]{2,1,0:T(8,128)}, f32[2,8,768]{2,...) custom-call(bf16[3,197,2,768]{3,2,1,0:T(2,128)(2,1)} %bitcast.7, ...), custom_call_target="tpu_custom_call" | custom-call | tf_op jit(solution)/shard_map/attn_back/pallas_call | solution.py:1350
  176.0 7.7 %collect.1 = (bf16[3,197,2,768]{3,2,1,0:T(2,128)(2,1)}, f32[3,197,2,768]{3,2,1,0:T(2,128)}, f32[96,192]{1,0:T(8,128)}, f32[96,576]{1,0:T(8,128)}, f32[96,192]{1,...) custom-call(f32[2,32,768]{2,1,0:T(8,128)} %get-tuple-element.71.done, ...), custom_call_target="tpu_custom_call" | custom-call | tf_op jit(solution)/shard_map/collect/pallas_call | solution.py:1393
where the time goes:
time: 184 us
  Pallas kernels  183 us (99%)
    pallas_call x1, Pallas kernels, on_device(): pl.pallas_call(functools.partial(attn_back_kernel, F, V, videos_here, fra...  81.7 us
    pallas_call x1, Pallas kernels, on_device(): pl.pallas_call(functools.partial(mlp_kernel, F, V, videos_here, frames_he...  63.5 us
    pallas_call x1, Pallas kernels, on_device(): pl.pallas_call(functools.partial(attn_fwd_kernel, F, V, frames_here, vide...  30.1 us
    pallas_call x1, Pallas kernels, on_device(): pl.pallas_call(functools.partial(collect_kernel, F, V, videos_here, frame...  7.73 us

commit v1 on v0

--- a/solution.py
+++ b/solution.py
@@ -79,14 +79,12 @@
     low = low_half()
     scaled = grad * inv
     scaled_low = scaled.astype(BF)
-    both = mixed.astype(F32) * scaled
-    zero = jnp.zeros_like(both)
+    minus = -pltpu.roll(mixed.astype(F32) * scaled, 64, 1)
     totals = None
     for head in range(2):
         p = probs(head)
-        grad_p = dims(scaled_low, half(low, head, v, jnp.zeros_like(v)), 1, 1)
-        delta = jnp.sum(half(low, head, both, zero), axis=1, keepdims=True)
-        grad_s = (p.astype(F32) * (grad_p - delta)).astype(BF)
+        centred = dims(half(low, head, scaled, minus).astype(BF), half(low, head, v, jnp.ones_like(v)), 1, 1)
+        grad_s = (p.astype(F32) * centred).astype(BF)
         terms = (
             dims(grad_s, half(low, head, k, jnp.zeros_like(k)), 1, 0),
             dims(grad_s, half(low, head, q, jnp.zeros_like(q)), 0, 0),
@@ -617,11 +615,11 @@
 
 def mlp_kernel(
     frame_size, video_size, videos_here, frames_here,
-    kept_ref, cot_ref, gain, shift, fc_bias, proj_bias, fc_hbm, proj_hbm,
-    out_ref, grad_ref, done_ref, mid_ref, raw_hbm, sums,
-    wide, normed2, cot2, act, grad_h, out_acc, grad_acc, bias_rows, bias_sums, fc_buf, proj_buf, fc_all,
+    kept_hbm, cot_hbm, gain, shift, fc_bias, proj_bias, fc_hbm, proj_hbm,
+    out_hbm, grad_hbm, done_ref, mid_ref, raw_hbm, sums,
+    kept_ref, cot_ref, grad_ref, wide, normed2, cot2, act, grad_h, out_acc, grad_acc, bias_rows, bias_sums, fc_buf, proj_buf, fc_all,
     grads, recv0, recv_a, recv_b, recv_c, send3, recv3,
-    s_load, s_raw, s_send0, s_recv0, s_sendb, s_recvb, s_send3, s_recv3,
+    s_rows, s_load, s_raw, s_send0, s_recv0, s_sendb, s_recvb, s_send3, s_recv3,
 ):
     chunk = pl.program_id(0)
     frames = videos_here * frames_here
@@ -649,12 +647,29 @@
                 out.append(pltpu.make_async_copy(fc_hbm.at[:, pl.ds(at, wide_step)], fc_buf.at[slot, :, to], s_load.at[slot, 1, f]))
         return out
 
+    def row_loads(i):
+        part = pl.ds(i * frames_here, frames_here)
+        return [
+            pltpu.make_async_copy(kept_hbm.at[part], kept_ref.at[part], s_rows.at[0, i]),
+            pltpu.make_async_copy(cot_hbm.at[i], cot_ref.at[i], s_rows.at[1, i]),
+        ]
+
+    def row_stores(i):
+        part = pl.ds(i * frames_here, frames_here)
+        return [
+            pltpu.make_async_copy(grad_ref.at[part], grad_hbm.at[part], s_rows.at[0, i]),
+            pltpu.make_async_copy(cot_ref.at[i], out_hbm.at[i], s_rows.at[1, i]),
+        ]
+
     def load_all():
         return pltpu.make_async_copy(fc_hbm, fc_all, s_load.at[0, 1, 0])
 
     @pl.when(chunk == 0)
     def _():
         place.announce()
+        for n in range(videos_here):
+            for load in row_loads(n):
+                load.start()
         for load in loads(chunk):
             load.start()
         if not sliced:
@@ -670,6 +685,8 @@
 
         @pl.loop(0, videos_here)
         def _(i):
+            for load in row_loads(i):
+                load.wait()
             cot = cot_ref[i].astype(F32)
             for j in range(frames_here):
                 wide[j, 0:PATCHES, :] = cot[:, j, :]
@@ -795,16 +812,18 @@
         @pl.loop(0, videos_here)
         def _(i):
             outs = [out_acc[rows_of(i * frames_here + j), :][:PATCHES] for j in range(frames_here)]
-            out_ref[i] = jnp.stack(outs, axis=1).astype(BF)
-
-        @pl.loop(0, frames)
-        def _(b):
-            rows = rows_of(b)
-            _, unit, inv = norm_fwd(kept_ref[b], vec(gain), vec(shift))
+            cot_ref[i] = jnp.stack(outs, axis=1).astype(BF)
+            every = frames_here * ROWS
+            here = pl.ds(i * frames_here, frames_here)
+            rows = rows_of(i, frames_here)
+            _, unit, inv = norm_fwd(kept_ref[here].reshape(every, D), vec(gain), vec(shift))
             grad = grad_acc[rows, :]
             sums[0:1, :] += column_sum(grad * unit)
             sums[1:2, :] += column_sum(grad)
-            grad_ref[b] = norm_back(grad, unit, inv, vec(gain)) + cot2[rows, :].astype(F32)
+            grad = norm_back(grad, unit, inv, vec(gain)) + cot2[rows, :].astype(F32)
+            grad_ref[here] = grad.reshape(frames_here, ROWS, D)
+            for store in row_stores(i):
+                store.start()
 
         @pl.loop(0, 2)
         def _(unit):
@@ -813,17 +832,20 @@
 
         pl.loop(0, 4)(lambda unit: scatter.drain(unit, source(unit)))
         raw().wait()
+        for n in range(videos_here):
+            for store in row_stores(n):
+                store.wait()
 
 
 def attn_back_kernel(
     frame_size, video_size, videos_here, frames_here,
-    x_hbm, normed_hbm, w_in_hbm, msg_ref, gk_ref, gain, shift, w_out, mlp_sums, mid_ref, raw_hbm, cls_ref, *rest,
+    x_hbm, normed_hbm, w_in_hbm, gk_hbm, mixed_hbm, msg_ref, gain, shift, w_out, mlp_sums, mid_ref, raw_hbm, cls_ref, *rest,
 ):
     msg_operands, rest = rest[:8], rest[8:]
     (
-        mixed_ref, q_ref, k_ref, v_ref, p_ref, inv_ref,
+        q_ref, k_ref, v_ref, p_ref, inv_ref,
         tg_ref, reduced_ref, near_ref, far_ref, totals_ref, msg_ref_out, in_ref_out, out_ref_out, msg_sums, grad_cls,
-        x_ref, normed_ref, w_in, joined, staged, gqkv_all, gk_all, sums, gm_grads, gm_wide, gm_own, gm_rows, gm_all, wide, cls_grads,
+        x_ref, normed_ref, w_in, gk_ref, mixed_ref, joined, staged, gqkv_all, gk_all, sums, gm_grads, gm_wide, gm_own, gm_rows, gm_all, wide, cls_grads,
         acc_mlp, *rest,
     ) = rest
     last_buffers, rest = rest[:6], rest[6:]
@@ -832,7 +854,7 @@
     (vec_near, vec_mid, vec_far), rest = rest[:3], rest[3:]
     msg_kept, (msg_gqkv, msg_mixed), msg_state, rest = list(rest[:7]), rest[7:9], rest[9:15], rest[15:]
     msg_kept.insert(6, gqkv_all.at[0:D])
-    (s_late, s_msg, s_local, s_staged, s_vsend, s_vrecv, s_gsend, s_grecv), rest = rest[:8], rest[8:]
+    (s_rows, s_late, s_msg, s_local, s_staged, s_vsend, s_vrecv, s_gsend, s_grecv), rest = rest[:9], rest[9:]
     names = ("send0", "recv0", "send_bits", "recv_bits", "send3", "recv3")
     last_sems, near_sems, far_sems = (dict(zip(names, rest[6 * i : 6 * i + 6])) for i in range(3))
     frames = videos_here * frames_here
@@ -865,6 +887,12 @@
     def msg_loads():
         return [pltpu.make_async_copy(a, b, s_msg.at[i]) for i, (a, b) in enumerate(zip(msg_operands, msg_kept))]
 
+    def row_loads(c):
+        return [
+            pltpu.make_async_copy(gk_hbm.at[c], gk_ref.at[c], s_rows.at[0, c]),
+            pltpu.make_async_copy(mixed_hbm.at[c], mixed_ref.at[c], s_rows.at[1, c]),
+        ]
+
     def late_loads():
         out = [
             pltpu.make_async_copy(x_hbm, x_ref, s_late.at[0]), pltpu.make_async_copy(normed_hbm, normed_ref, s_late.at[1]),
@@ -880,7 +908,14 @@
         pl.when(t == min(at, steps - 1))(call)
 
     def begin():
-        place.greet()
+        place.announce()
+
+        @pl.loop(0, frames)
+        def _(c):
+            for load in row_loads(c):
+                load.start()
+
+        place.meet()
         sums[...] = jnp.zeros_like(sums)
 
         @each_last
@@ -919,12 +954,13 @@
     due(6, lambda: each_last(lasts.middle))
     due(8, land_lasts)
     due(frames + 2, lambda: each_attn(lambda unit: near.stage(unit, 0)))
-    due(steps - 1, lambda: each_last(lasts.finish))
     rows = pl.ds(pl.multiple_of(b * ROWS, ROWS), ROWS)
     side_lanes = pl.ds(pl.multiple_of(side * HALF, HALF), HALF)
 
     @pl.when(side == 0)
     def _():
+        for load in row_loads(b):
+            load.wait()
         gk_low = gk_ref[b].astype(BF)
         gk_all[b] = gk_low
         sums[0:1, :] += column_sum(gk_low.astype(F32))
@@ -974,8 +1010,8 @@
         for c in range(frames):
             piece = gqkv_all[c * ROWS + at : c * ROWS + at + 16, :].astype(F32)
             gm_grads[c : c + 1, :] = piece[PATCHES - at : PATCHES - at + 1]
-            joined[c : c + 1, :] = msg_ref[c]
-        _, unit, inv = norm_fwd(joined[0:frames, :], vec(gain), vec(shift))
+            joined[0, c : c + 1, :] = msg_ref[c]
+        _, unit, inv = norm_fwd(joined[0, 0:frames, :], vec(gain), vec(shift))
         grad = dims(gm_grads[...].astype(BF), w_in[...], 1, 1)[0:frames]
         gm_wide[0:frames, :] = norm_back(grad, unit, inv, vec(gain))
         for i in range(videos_here):
@@ -984,6 +1020,7 @@
         gather.start()
         each_attn(near.middle)
         attn_units(1, acc_far, far)
+        each_last(lasts.finish)
         early.finish()
         gather.near()
         gather.forward()
@@ -994,19 +1031,26 @@
         def norm_frames(lo, hi):
             @pl.loop(lo, hi)
             def _(i):
+                @pl.when(i > 0)
+                def _():
+                    for j in range(frames_here):
+                        put(i - 1, j).wait()
+
                 x = x_ref[i].astype(F32)
+                first = i * frames_here
                 for j in range(frames_here):
-                    c = i * frames_here + j
-                    joined[0:PATCHES, :] = x[:, j, :]
-                    joined[PATCHES:ROWS, :] = jnp.zeros((ROWS - PATCHES, D), F32)
-                    joined[PATCHES : PATCHES + 1, :] = msg_ref[c]
-                    _, unit, inv = norm_fwd(joined[...], vec(gain), vec(shift))
-                    rows = pl.ds(pl.multiple_of(c * ROWS, ROWS), ROWS)
-                    grad = dims(gqkv_all[rows, :], w_in[...], 1, 1)
-                    sums[3:4, :] += column_sum(grad * unit)
-                    sums[4:5, :] += column_sum(grad)
-                    pl.when(i > 0)(lambda j=j: put(i - 1, j).wait())
-                    staged[j] = (gk_ref[c] + norm_back(grad, unit, inv, vec(gain)))[:PATCHES]
+                    joined[j, 0:PATCHES, :] = x[:, j, :]
+                    joined[j, PATCHES:ROWS, :] = jnp.zeros((ROWS - PATCHES, D), F32)
+                    joined[j, PATCHES : PATCHES + 1, :] = msg_ref[first + j]
+                every = frames_here * ROWS
+                rows = pl.ds(pl.multiple_of(first * ROWS, ROWS), every)
+                grad = dims(gqkv_all[rows, :], w_in[...], 1, 1)
+                _, unit, inv = norm_fwd(joined[...].reshape(every, D), vec(gain), vec(shift))
+                sums[3:4, :] += column_sum(grad * unit)
+                sums[4:5, :] += column_sum(grad)
+                back = gk_ref[pl.ds(first, frames_here)].reshape(every, D) + norm_back(grad, unit, inv, vec(gain))
+                for j in range(frames_here):
+                    staged[j] = back[j * ROWS : j * ROWS + PATCHES]
                     put(i, j).start()
 
         norm_frames(0, 1)
@@ -1034,16 +1078,20 @@
                         wide[at_row : at_row + frames_here, :] = gm_rows[video, i, f].astype(F32)
                 gm_all[video * count : video * count + count, :] = wide[...].astype(BF)
 
+        def after():
+            pass
+
         blocks = video_size * count // BLOCK
         if blocks > 1:
             between()
+            after()
 
         @pl.loop(0, blocks)
         def _(block):
             at = pl.ds(pl.multiple_of(block * BLOCK, BLOCK), BLOCK)
             msg_back_block(
                 place, cls_ref[at, :], gm_all.at[at], msg_kept, msg_ref_out, in_ref_out, out_ref_out, msg_sums, cls_grads.at[at],
-                msg_state, msg_gqkv, msg_mixed, between if blocks == 1 else lambda: None,
+                msg_state, msg_gqkv, msg_mixed, *((between, after) if blocks == 1 else (lambda: None,) * 2),
             )
 
         for i in range(videos_here):
@@ -1064,7 +1112,7 @@
                 scatter.drain_video(unit)
 
 
-def msg_back_block(place, cls, gm_ref, kept, acc_msg, acc_in, acc_out, sums, cls_grad, scratch, gqkv, grad_mixed, between):
+def msg_back_block(place, cls, gm_ref, kept, acc_msg, acc_in, acc_out, sums, cls_grad, scratch, gqkv, grad_mixed, between, after):
     bias, gain, shift, in_bias, out_bias, w_msg, w_in, w_out = kept
     qkv, probs, invs, mixed, normed, _ = scratch
     own_rows = D // place.F
@@ -1073,14 +1121,14 @@
     def own_columns(x):
         return pltpu.roll(x.astype(F32), lax.rem(D - place.f * own_rows, D), 1)[:, :padded].astype(BF)
 
-    unit, inv_std = msg_forward(cls, (bias, gain, shift, in_bias, out_bias), w_msg, w_in, w_out, scratch, PAIRS // 2)
+    unit, inv_std = msg_forward(cls, (bias, gain, shift, in_bias, out_bias), w_msg, w_in, w_out, scratch, PAIRS)
     between()
     gm = gm_ref[...]
     acc_out[...] += dims(own_columns(mixed[...]), gm, 0, 0)
     sums[5:6, :] += column_sum(gm.astype(F32))
     grad_mixed[...] = dims(gm, w_out[...], 1, 1)
 
-    @pl.loop(0, PAIRS, unroll=PAIRS // 2)
+    @pl.loop(0, PAIRS, unroll=PAIRS)
     def _(pair):
         at = pair_lanes(pair)
         grads = pair_back(
@@ -1090,6 +1138,7 @@
         for kind in range(3):
             gqkv[:, pair_lanes(pair, kind)] = grads[kind].astype(BF)
 
+    after()
     own_normed = own_columns(normed[...])
     grad = None
     for kind in range(3):
@@ -1310,10 +1359,11 @@
     output, grad_kept, done, mid, raw, mlp_sums = pl.pallas_call(
         functools.partial(mlp_kernel, F, V, videos_here, frames_here),
         grid=(UNITS,),
-        in_specs=wholes(kept, cot, norm2_gain, norm2_shift, fc_bias, proj_bias) + [in_hbm(), in_hbm()],
-        out_specs=wholes(*mlp_outs[:4]) + [in_hbm()] + wholes(mlp_outs[5]),
+        in_specs=[in_hbm()] * 2 + wholes(norm2_gain, norm2_shift, fc_bias, proj_bias) + [in_hbm()] * 2,
+        out_specs=[in_hbm()] * 2 + wholes(*mlp_outs[2:4]) + [in_hbm()] + wholes(mlp_outs[5]),
         out_shape=mlp_outs,
         scratch_shapes=[
+            pltpu.VMEM(kept.shape, F32), pltpu.VMEM(x.shape, BF), pltpu.VMEM(kept.shape, F32),
             pltpu.VMEM((frames_here, ROWS, D), F32),
             pltpu.VMEM((total, D), BF), pltpu.VMEM((total, D), BF), pltpu.VMEM((total, width), BF), pltpu.VMEM((total, width), BF),
             pltpu.VMEM((total, D), F32), pltpu.VMEM((total, D), F32),
@@ -1323,7 +1373,7 @@
             pltpu.VMEM((2 * UNITS, 2) + block_shape, BF), pltpu.VMEM((4,) + block_shape, BF),
         ]
         + bit_buffers(4) + unit_buffers(2, [part_shape] * 2)
-        + [DMA((2, 2, F)), DMA((1,))] + exchange_sems(4),
+        + [DMA((2, videos_here)), DMA((2, 2, F)), DMA((1,))] + exchange_sems(4),
         compiler_params=params(63, collective_id=2, has_side_effects=True),
         name="mlp",
     )(kept, cot, norm2_gain, norm2_shift, fc_bias, proj_bias, fc_weight, proj_weight)
@@ -1350,15 +1400,16 @@
     tg, reduced, near, far, totals, acc_msg, acc_in, acc_out, msg_sums, grad_cls = pl.pallas_call(
         functools.partial(attn_back_kernel, F, V, videos_here, frames_here),
         grid=(2 * frames,),
-        in_specs=[in_hbm()] * 3
-        + wholes(msg_out, grad_kept, norm1_gain, norm1_shift, attn_out_weight, mlp_sums, mid)
-        + [in_hbm()] + wholes(cls) + [in_hbm()] * 8 + wholes(mixed)
+        in_specs=[in_hbm()] * 5
+        + wholes(msg_out, norm1_gain, norm1_shift, attn_out_weight, mlp_sums, mid)
+        + [in_hbm()] + wholes(cls) + [in_hbm()] * 8
         + [by_pairs(shape) for shape in ((ROWS, 128), (KEYS, 128), (KEYS, 128), (ROWS, 2 * KEYS), (ROWS, 128))],
         out_specs=[in_hbm()] + wholes(*back_outs[1:]),
         out_shape=back_outs,
         scratch_shapes=[
             pltpu.VMEM(x.shape, BF), pltpu.VMEM(normed.shape, BF), pltpu.VMEM((D, 3 * D), BF),
-            pltpu.VMEM((ROWS, D), F32), pltpu.VMEM((frames_here, PATCHES, D), F32),
+            pltpu.VMEM(grad_kept.shape, F32), pltpu.VMEM(mixed.shape, BF),
+            pltpu.VMEM((frames_here, ROWS, D), F32), pltpu.VMEM((frames_here, PATCHES, D), F32),
             pltpu.VMEM((max(total, D), 3 * D), BF), pltpu.VMEM((frames, ROWS, D), BF), pltpu.VMEM((8, D), F32), pltpu.VMEM((16, 3 * D), F32), pltpu.VMEM((8, D), F32),
             pltpu.VMEM((videos_here, frames_here, D), BF), pltpu.VMEM((V, videos_here, F, frames_here, D), BF),
             pltpu.VMEM((msgs, D), BF), pltpu.VMEM((group, D), F32), pltpu.VMEM((msgs, D), F32),
@@ -1369,14 +1420,14 @@
         + [pltpu.VMEM((2, F, 8, D), F32), pltpu.VMEM((2, 8, D), F32), pltpu.VMEM((2, V, 8, D), F32)]
         + [pltpu.VMEM(a.shape, BF) for a in msg_arrays if a is not msg_in_weight]
         + [pltpu.VMEM((BLOCK, 3 * D), BF), pltpu.VMEM((BLOCK, D), F32)] + msg_scratch(BLOCK)
-        + [DMA((8,)), DMA((8,)), DMA((2,)), DMA((frames_here,))]
+        + [DMA((2, frames)), DMA((8,)), DMA((8,)), DMA((2,)), DMA((frames_here,))]
         + [DMA((2, 2, max(F, V))), DMA((2, 2, max(F, V))), DMA((V, F + V)), DMA((V, F + V))]
         + exchange_sems(4) + exchange_sems(UNITS) + exchange_sems(UNITS),
         compiler_params=params(63, collective_id=3, has_side_effects=True),
         name="attn_back",
     )(
-        x, normed, attn_in_weight, msg_out, grad_kept, norm1_gain, norm1_shift, attn_out_weight, mlp_sums, mid, raw, cls,
-        *msg_arrays, mixed, q, k, v, p, inv,
+        x, normed, attn_in_weight, grad_kept, mixed, msg_out, norm1_gain, norm1_shift, attn_out_weight, mlp_sums, mid, raw, cls,
+        *msg_arrays, q, k, v, p, inv,
     )
 
     out_shapes = [

time: 184 us -> 177 us (0.962)
  Pallas kernels: 183 us -> 176 us
    pallas_call x1, Pallas kernels: 81.7 us -> 75.4 us  [on_device(): pl.pallas_call(functools.partial(attn_back_kernel, F, V, videos_here, fra...]
where the time goes in v1:
time: 177 us
  Pallas kernels  176 us (99%)
    pallas_call x1, Pallas kernels, on_device(): pl.pallas_call(functools.partial(attn_back_kernel, F, V, videos_here, fra...  75.4 us
    pallas_call x1, Pallas kernels, on_device(): pl.pallas_call(functools.partial(mlp_kernel, F, V, videos_here, frames_he...  62.9 us
    pallas_call x1, Pallas kernels, on_device(): pl.pallas_call(functools.partial(attn_fwd_kernel, F, V, frames_here, vide...  30.1 us
    pallas_call x1, Pallas kernels, on_device(): pl.pallas_call(functools.partial(collect_kernel, F, V, videos_here, frame...  7.73 us

profile of v1, /device:TPU:0, one launch (start us, length us, event | category | flops | bytes accessed | tf_op | source)
XLA Modules:
  0.0 177.0 jit_solution(9980588033496884304)
XLA Ops:
  0.7 30.1 %attn_fwd.1 = (bf16[6,6,208,128]{3,2,1,0:T(8,128)(2,1)}, bf16[6,6,256,128]{3,2,1,0:T(8,128)(2,1)}, bf16[6,6,256,128]{3,2,1,0:T(8,128)(2,1)}, bf16[6,208,768]{2,1...) custom-call(bf16[3,197,2,768]{3,2,1,0:T(2,128)(2,1)} %bitcast.5, ...), custom_call_target="tpu_custom_call" | custom-call | tf_op jit(solution)/shard_map/attn_fwd/pallas_call | solution.py:1317
  30.8 62.9 %mlp.1 = (bf16[3,197,2,768]{3,2,1,0:T(2,128)(2,1)}, f32[6,208,768]{2,1,0:T(8,128)}, f32[2,32,768]{2,1,0:T(8,128)}, bf16[2,32,3072]{2,1,0:T(8,128)(2,1)}, bf16[2,...) custom-call(f32[6,208,768]{2,1,0:T(8,128)} %get-tuple-element.70.kept_hbm, bf16[3,197,2,768]{3,2,1,0:T(2,128)(2,1)} %bitcast.8, ...), custom_call_target="tpu_custom_call" | custom-call | tf_op jit(solution)/shard_map/mlp/pallas_call | solution.py:1359
  93.7 75.4 %attn_back.1 = (f32[3,197,2,768]{3,2,1,0:T(2,128)}, f32[4,32,768]{2,1,0:T(8,128)}, f32[3,32,576]{2,1,0:T(8,128)}, f32[3,32,384]{2,1,0:T(8,128)}, f32[2,8,768]{2,...) custom-call(bf16[3,197,2,768]{3,2,1,0:T(2,128)(2,1)} %bitcast.7, ...), custom_call_target="tpu_custom_call" | custom-call | tf_op jit(solution)/shard_map/attn_back/pallas_call | solution.py:1400
  169.1 7.7 %collect.1 = (bf16[3,197,2,768]{3,2,1,0:T(2,128)(2,1)}, f32[3,197,2,768]{3,2,1,0:T(2,128)}, f32[96,192]{1,0:T(8,128)}, f32[96,576]{1,0:T(8,128)}, f32[96,192]{1,...) custom-call(f32[2,32,768]{2,1,0:T(8,128)} %get-tuple-element.71.done, ...), custom_call_target="tpu_custom_call" | custom-call | tf_op jit(solution)/shard_map/collect/pallas_call | solution.py:1444

commit v2 on v1

--- a/solution.py
+++ b/solution.py
@@ -480,7 +480,7 @@
 
     def add(self, unit, block, came):
         target = self.acc(unit, block)
-        target[...] = (target[...].astype(F32) + came.astype(F32)).astype(BF)
+        target[...] = target[...] + came
 
     def stage(self, unit, stage):
         if stage == 0:
@@ -702,7 +702,6 @@
 
         if not sliced:
             load_all().wait()
-        place.meet()
 
     for load in loads(chunk):
         load.wait()
@@ -739,6 +738,7 @@
 
     @pl.loop(0, tiles)
     def _(t):
+        due(0, 2, t, place.meet)
         due(1, 1, t, both(lambda unit: scatter.stage(unit, 0), 0))
         due(2, 0, t, both(scatter.middle, 0))
         due(2, 1, t, both(lambda unit: scatter.stage(unit, 0), 2))
@@ -758,8 +758,7 @@
 
     unit = 2 * chunk
 
-    @pl.loop(0, 2)
-    def _(m):
+    def weight_grads(m):
         size = width // 2
         count = frame_size // 4
         value = dims(act[:, pl.ds(pl.multiple_of(m * size, size), size)], cot2[...], 0, 0).astype(BF)
@@ -769,18 +768,16 @@
                 grads[
                     unit + 1, lax.rem(core + place.core, 2), pl.ds(m * count, count), :, q * D : q * D + D
                 ] = value[:, core, q]
-
-    @pl.loop(0, 2)
-    def _(m):
         size = D // 2
         value = dims(normed2[:, pl.ds(pl.multiple_of(m * size, size), size)], grad_h[...], 0, 0).astype(BF)
-        count = frame_size // 4
         value = value.reshape(count, 2, UNITS, step, width)
         for core in range(2):
             for q in range(UNITS):
                 grads[
                     unit, lax.rem(core + place.core, 2), pl.ds(m * count, count), :, q * width : q * width + width
                 ] = value[:, core, q]
+
+    pl.loop(0, 2)(weight_grads)
 
     def raw():
         return pltpu.make_async_copy(grads.at[pl.ds(4, 2)], raw_hbm, s_raw.at[0])
@@ -915,20 +912,18 @@
             for load in row_loads(c):
                 load.start()
 
-        place.meet()
         sums[...] = jnp.zeros_like(sums)
-
-        @each_last
-        def _(unit):
-            lasts.exchange0(unit, last_source(unit)).start()
-            local(unit).start()
-
-        early.start()
+        each_last(lambda unit: local(unit).start())
         for load in late_loads():
             load.start()
         for at, load in enumerate(msg_loads()):
             if at != 6:
                 load.start()
+
+    def begin_far():
+        place.meet()
+        each_last(lambda unit: lasts.exchange0(unit, last_source(unit)).start())
+        early.start()
         for unit in range(2):
             lasts.send_video(unit, MLP_PARTS[unit], mid_ref[unit])
 
@@ -948,12 +943,6 @@
             scatter.send_video(unit, attn_parts(group), scatter.land(unit)[...])
 
     due(0, begin)
-    due(2, open_lasts)
-    due(4, lambda: each_mid(lasts.finish))
-    due(5, early.forward)
-    due(6, lambda: each_last(lasts.middle))
-    due(8, land_lasts)
-    due(frames + 2, lambda: each_attn(lambda unit: near.stage(unit, 0)))
     rows = pl.ds(pl.multiple_of(b * ROWS, ROWS), ROWS)
     side_lanes = pl.ds(pl.multiple_of(side * HALF, HALF), HALF)
 
@@ -975,6 +964,13 @@
         for kind in range(3):
             at = pl.ds(pl.multiple_of((side * 3 + kind) * HALF + pair * 128, 128), 128)
             gqkv_all[rows, at] = grads[kind][:ROWS].astype(BF)
+    due(0, begin_far)
+    due(1, open_lasts)
+    due(3, lambda: each_mid(lasts.finish))
+    due(4, early.forward)
+    due(5, lambda: each_last(lasts.middle))
+    due(7, land_lasts)
+    due(frames + 1, lambda: each_attn(lambda unit: near.stage(unit, 0)))
     for row, kind in ((1, 0), (2, 2)):
         part = gqkv_all[rows, pl.ds(pl.multiple_of((side * 3 + kind) * HALF, HALF), HALF)]
         sums[row : row + 1, side_lanes] += column_sum(part.astype(F32))
@@ -1161,13 +1157,19 @@
 
 def collect_kernel(
     frame_size, video_size, videos_here, frames_here,
-    done, reduced, near, far, totals, acc_msg, acc_in, acc_out, sums, grad_cls, tg_hbm, output_hbm,
-    output, tokens_grad, msg_grad, in_grad, out_grad, *rest,
+    *rest,
+):
+    small, (tg_hbm, output_hbm, output, tokens_grad, *rest) = rest[:10], rest[10:]
+    collect(frame_size, video_size, videos_here, frames_here, small, tg_hbm, output_hbm, output, tokens_grad, *rest)
+
+
+def collect(
+    frame_size, video_size, videos_here, frames_here, small, tg_hbm, output_hbm, output, tokens_grad, msg_grad, in_grad, out_grad, *rest,
 ):
     (
         msg_bias_g, msg_gain_g, msg_shift_g, msg_in_bias_g, msg_out_bias_g, gain1_g, shift1_g,
         attn_in_g, attn_in_bias_g, attn_out_g, attn_out_bias_g, gain2_g, shift2_g, fc_g, fc_bias_g, proj_g, proj_bias_g,
-        tg, out, sem,
+        tg, out, sem, s_small, *kept,
     ) = rest
     f, v = lax.axis_index("frame"), lax.axis_index("video")
     own_rows = D // frame_size
@@ -1187,6 +1189,12 @@
     for i in range(videos_here):
         load(i).start()
         load_out(i).start()
+    smalls = [pltpu.make_async_copy(a, b, s_small.at[at]) for at, (a, b) in enumerate(zip(small, kept))]
+    for copy in smalls:
+        copy.start()
+    for copy in smalls:
+        copy.wait()
+    done, reduced, near, far, totals, acc_msg, acc_in, acc_out, sums, grad_cls = kept
     for i in range(videos_here):
         load(i).wait()
         added = [grad_cls[i * frames_here + j] for j in range(frames_here)]
@@ -1444,10 +1452,11 @@
     ) = pl.pallas_call(
         functools.partial(collect_kernel, F, V, videos_here, frames_here),
         grid=(1,),
-        in_specs=wholes(done, reduced, near, far, totals, acc_msg, acc_in, acc_out, msg_sums, grad_cls) + [in_hbm()] * 2,
+        in_specs=[in_hbm()] * 12,
         out_specs=[in_hbm()] * 2 + wholes(*out_shapes),
         out_shape=[shaped(x.shape, BF), shaped(x.shape, F32)] + out_shapes,
-        scratch_shapes=[pltpu.VMEM(x.shape, F32), pltpu.VMEM(x.shape, BF), DMA((2, videos_here))],
+        scratch_shapes=[pltpu.VMEM(x.shape, F32), pltpu.VMEM(x.shape, BF), DMA((2, videos_here)), DMA((10,))]
+        + [pltpu.VMEM(a.shape, F32) for a in (done, reduced, near, far, totals, acc_msg, acc_in, acc_out, msg_sums, grad_cls)],
         compiler_params=params(63),
         name="collect",
     )(done, reduced, near, far, totals, acc_msg, acc_in, acc_out, msg_sums, grad_cls, tg, output)

time: 177 us -> 175 us (0.989)
  Pallas kernels: 176 us -> 174 us
where the time goes in v2:
time: 175 us; the launch traced here: 174 us
  Pallas kernels  174 us (99%)
    pallas_call x1, Pallas kernels, on_device(): pl.pallas_call(functools.partial(attn_back_kernel, F, V, videos_here, fra...  74.8 us
    pallas_call x1, Pallas kernels, on_device(): pl.pallas_call(functools.partial(mlp_kernel, F, V, videos_here, frames_he...  61.5 us
    pallas_call x1, Pallas kernels, on_device(): pl.pallas_call(functools.partial(attn_fwd_kernel, F, V, frames_here, vide...  30.1 us
    pallas_call x1, Pallas kernels, on_device(): pl.pallas_call(functools.partial(collect_kernel, F, V, videos_here, frame...  7.11 us

profile of v2, /device:TPU:0, one launch (start us, length us, event | category | flops | bytes accessed | tf_op | source)
XLA Modules:
  0.0 174.4 jit_solution(10317680128459837462)
XLA Ops:
  0.7 30.1 %attn_fwd.1 = (bf16[6,6,208,128]{3,2,1,0:T(8,128)(2,1)}, bf16[6,6,256,128]{3,2,1,0:T(8,128)(2,1)}, bf16[6,6,256,128]{3,2,1,0:T(8,128)(2,1)}, bf16[6,208,768]{2,1...) custom-call(bf16[3,197,2,768]{3,2,1,0:T(2,128)(2,1)} %bitcast.5, ...), custom_call_target="tpu_custom_call" | custom-call | tf_op jit(solution)/shard_map/attn_fwd/pallas_call | solution.py:1325
  30.8 61.5 %mlp.1 = (bf16[3,197,2,768]{3,2,1,0:T(2,128)(2,1)}, f32[6,208,768]{2,1,0:T(8,128)}, f32[2,32,768]{2,1,0:T(8,128)}, bf16[2,32,3072]{2,1,0:T(8,128)(2,1)}, bf16[2,...) custom-call(f32[6,208,768]{2,1,0:T(8,128)} %get-tuple-element.70.kept_hbm, bf16[3,197,2,768]{3,2,1,0:T(2,128)(2,1)} %bitcast.8, ...), custom_call_target="tpu_custom_call" | custom-call | tf_op jit(solution)/shard_map/mlp/pallas_call | solution.py:1367
  92.3 74.8 %attn_back.1 = (f32[3,197,2,768]{3,2,1,0:T(2,128)}, f32[4,32,768]{2,1,0:T(8,128)}, f32[3,32,576]{2,1,0:T(8,128)}, f32[3,32,384]{2,1,0:T(8,128)}, f32[2,8,768]{2,...) custom-call(bf16[3,197,2,768]{3,2,1,0:T(2,128)(2,1)} %bitcast.7, ...), custom_call_target="tpu_custom_call" | custom-call | tf_op jit(solution)/shard_map/attn_back/pallas_call | solution.py:1408
  167.1 7.1 %collect.1 = (bf16[3,197,2,768]{3,2,1,0:T(2,128)(2,1)}, f32[3,197,2,768]{3,2,1,0:T(2,128)}, f32[96,192]{1,0:T(8,128)}, f32[96,576]{1,0:T(8,128)}, f32[96,192]{1,...) custom-call(f32[2,32,768]{2,1,0:T(8,128)} %get-tuple-element.71.rest, ...), custom_call_target="tpu_custom_call" | custom-call | tf_op jit(solution)/shard_map/collect/pallas_call | solution.py:1452

commit v3 on v2

--- a/solution.py
+++ b/solution.py
@@ -292,9 +292,10 @@
         normed_ref[here] = normed.astype(BF).reshape(frames_here, ROWS, D)
         normed = normed_ref[here].reshape(every, D)
         pad = jnp.zeros((KEYS - ROWS, 128), BF)
-        q = ((dims(normed, w_in1[:, :D], 1, 0) + vec(in_bias1)) * 0.125).astype(BF)
-        k = dims(normed, w_in1[:, D : 2 * D], 1, 0).astype(BF)
-        v = (dims(normed, w_in1[:, 2 * D :], 1, 0) + vec(in_bias1, 1)).astype(BF)
+        qkv = dims(normed, w_in1[...], 1, 0)
+        q = ((qkv[:, :D] + vec(in_bias1)) * 0.125).astype(BF)
+        k = qkv[:, D : 2 * D].astype(BF)
+        v = (qkv[:, 2 * D :] + vec(in_bias1, 1)).astype(BF)
         for j in range(frames_here):
             part = slice(j * ROWS, j * ROWS + ROWS)
             for pair in range(PAIRS):

time: 175 us -> 175 us (level)
  no operation moved by 1% of the time
where the time goes in v3:
time: 175 us; the launch traced here: 174 us
  Pallas kernels  174 us (99%)
    pallas_call x1, Pallas kernels, on_device(): pl.pallas_call(functools.partial(attn_back_kernel, F, V, videos_here, fra...  74.8 us
    pallas_call x1, Pallas kernels, on_device(): pl.pallas_call(functools.partial(mlp_kernel, F, V, videos_here, frames_he...  61.5 us
    pallas_call x1, Pallas kernels, on_device(): pl.pallas_call(functools.partial(attn_fwd_kernel, F, V, frames_here, vide...  30.1 us
    pallas_call x1, Pallas kernels, on_device(): pl.pallas_call(functools.partial(collect_kernel, F, V, videos_here, frame...  7.11 us

profile of v3, /device:TPU:0, one launch (start us, length us, event | category | flops | bytes accessed | tf_op | source)
XLA Modules:
  0.0 174.4 jit_solution(14827279902139161600)
XLA Ops:
  0.7 30.1 %attn_fwd.1 = (bf16[6,6,208,128]{3,2,1,0:T(8,128)(2,1)}, bf16[6,6,256,128]{3,2,1,0:T(8,128)(2,1)}, bf16[6,6,256,128]{3,2,1,0:T(8,128)(2,1)}, bf16[6,208,768]{2,1...) custom-call(bf16[3,197,2,768]{3,2,1,0:T(2,128)(2,1)} %bitcast.5, ...), custom_call_target="tpu_custom_call" | custom-call | tf_op jit(solution)/shard_map/attn_fwd/pallas_call | solution.py:1326
  30.8 61.5 %mlp.1 = (bf16[3,197,2,768]{3,2,1,0:T(2,128)(2,1)}, f32[6,208,768]{2,1,0:T(8,128)}, f32[2,32,768]{2,1,0:T(8,128)}, bf16[2,32,3072]{2,1,0:T(8,128)(2,1)}, bf16[2,...) custom-call(f32[6,208,768]{2,1,0:T(8,128)} %get-tuple-element.70.kept_hbm, bf16[3,197,2,768]{3,2,1,0:T(2,128)(2,1)} %bitcast.8, ...), custom_call_target="tpu_custom_call" | custom-call | tf_op jit(solution)/shard_map/mlp/pallas_call | solution.py:1368
  92.3 74.8 %attn_back.1 = (f32[3,197,2,768]{3,2,1,0:T(2,128)}, f32[4,32,768]{2,1,0:T(8,128)}, f32[3,32,576]{2,1,0:T(8,128)}, f32[3,32,384]{2,1,0:T(8,128)}, f32[2,8,768]{2,...) custom-call(bf16[3,197,2,768]{3,2,1,0:T(2,128)(2,1)} %bitcast.7, ...), custom_call_target="tpu_custom_call" | custom-call | tf_op jit(solution)/shard_map/attn_back/pallas_call | solution.py:1409
  167.1 7.1 %collect.1 = (bf16[3,197,2,768]{3,2,1,0:T(2,128)(2,1)}, f32[3,197,2,768]{3,2,1,0:T(2,128)}, f32[96,192]{1,0:T(8,128)}, f32[96,576]{1,0:T(8,128)}, f32[96,192]{1,...) custom-call(f32[2,32,768]{2,1,0:T(8,128)} %get-tuple-element.71.rest, ...), custom_call_target="tpu_custom_call" | custom-call | tf_op jit(solution)/shard_map/collect/pallas_call | solution.py:1453
